TPU v7x, 128 devices: a whole 4x4x4 slice. The times are simulated.
128 devices in a mesh: tm: 16 (over y, x_hi, core), inch: 8 (over z, x_lo).
Axes of the slice: x: 4 (x_hi: 2, x_lo: 2; x = x_hi * 2 + x_lo), y: 4, z: 4, core: 2. Of those that a mesh axis runs over, the one named last changes fastest.
Arguments:
- signal: bfloat16 [32768, 128], P('tm', 'inch'), may hold values from -6 to 6
- response: bfloat16 [32768, 256], P('tm'), may hold values from -6 to 6
- kernel: float32 [256, 128, 256], P('tm', 'inch'), may hold values from -16 to 16
Outputs:
- kernel_out: float32 [256, 128, 256], P('tm', 'inch')
- residual: bfloat16 [32768, 256], P('tm', 'inch')
All inputs are finite; a program needn't handle non-finite values.
Results may differ from a plain program's by a relative error of at most 0.024.
Values may be sent and summed in bfloat16 or wider, within the bound.
A program may use at most 576 MiB of HBM per device.

v0:
```python
import math

import jax
import jax.numpy as jnp
from jax import lax
from jax.experimental import pallas as pl
from jax.experimental.pallas import tpu as pltpu
from jax.sharding import PartitionSpec as P

STEP_SIZE = 0.5
EPSILON = 1e-06
F32 = jnp.float32
BF16 = jnp.bfloat16
MESH = pl.DeviceIdType.MESH
TAPS = 256
CI = 128
CO = 256
SCALE = 1.0 / math.sqrt(TAPS * CI)
COUNT = TAPS * CI * CO


def remote(src, dst, send, recv, device):
    return pltpu.make_async_remote_copy(
        src_ref=src, dst_ref=dst, send_sem=send, recv_sem=recv,
        device_id=device, device_id_type=MESH,
    )


def body(
    sig_ref, tail_ref, ker_ref, resp_ref,
    step_ref, resid_ref,
    pieces, halo_in, perm, sb, xe, weights, response, r_even, r_odd,
    grad_out, grad_in, grad_own, grad_all, tiles, energy_a, energy_b, energy_own, acc, resid_all,
    resid_in,
    ker_send, ker_recv, resp_send, resp_recv, tail_send, tail_recv,
    z_send, z_recv, zh_send, zh_recv, x_send, x_recv, c_send, c_recv,
    w_send, w_recv, rs_send, rs_recv, ag_send, ag_recv,
    ea_send, ea_recv, eb_send, eb_recv, t_send, t_recv, o_send, o_recv,
):
    tm = lax.axis_index("tm")
    inch = lax.axis_index("inch")
    y = tm // 4
    s = tm % 4
    x_hi = s // 2
    core = s % 2
    z = inch // 2
    x_lo = inch % 2
    x = x_hi * 2 + x_lo
    rank = inch * 4 + s

    def in_plane(d):
        return (y * 4 + d % 4, d // 4)

    def along_y(r):
        return ((((y + r) % 4) * 4) + s, inch)

    def along_z(r):
        return (tm, ((z + r) % 4) * 2 + x_lo)

    def along_x(r):
        there = (x + r) % 4
        return (y * 4 + (there // 2) * 2 + core, z * 2 + there % 2)

    def in_group(r):
        return (y * 4 + (s + r) % 4, inch)

    barrier = pltpu.get_barrier_semaphore()

    def greet(r, carry):
        pl.semaphore_signal(
            barrier, inc=1, device_id=in_plane((rank + r) % 32), device_id_type=MESH
        )
        return carry

    lax.fori_loop(1, 32, greet, 0)
    for r in (1, 2, 3):
        pl.semaphore_signal(barrier, inc=1, device_id=along_y(r), device_id_type=MESH)
    pl.semaphore_signal(
        barrier, inc=1, device_id=((tm + 15) % 16, inch), device_id_type=MESH
    )

    lane_z = pl.ds(pl.multiple_of(z * 128, 128), 128)
    pieces[x_hi, core, x_lo, 0:256, lane_z] = sig_ref[...]

    pl.semaphore_wait(barrier, 35)

    tail_copy = remote(tail_ref, halo_in, tail_send, tail_recv, ((tm + 1) % 16, inch))
    tail_copy.start()
    z_copies = []
    for r in (1, 2, 3):
        view = pieces.at[x_hi, core, x_lo, pl.ds(0, 256), lane_z]
        z_copies.append(remote(view, view, z_send.at[r - 1], z_recv.at[r - 1], along_z(r)))
        z_copies[-1].start()

    row_k = pl.multiple_of((s // 2) * 128 + inch * 16, 16)
    lane_k = pl.multiple_of((s % 2) * 128, 128)

    def send_taps(r, carry):
        d = (rank + r) % 32
        remote(
            ker_ref.at[d], weights.at[y, pl.ds(row_k, 16), pl.ds(lane_k, 128)],
            ker_send, ker_recv, in_plane(d),
        ).start()
        return carry

    lax.fori_loop(1, 32, send_taps, 0)
    weights[y, pl.ds(row_k, 16), pl.ds(lane_k, 128)] = ker_ref[rank]

    tail_copy.wait()
    pieces[x_hi, core, x_lo, 256:288, lane_z] = halo_in[...]
    zh_copies = []
    for r in (1, 2, 3):
        view = pieces.at[x_hi, core, x_lo, pl.ds(256, 32), lane_z]
        zh_copies.append(remote(view, view, zh_send.at[r - 1], zh_recv.at[r - 1], along_z(r)))
        zh_copies[-1].start()

    rows_s = pl.ds(pl.multiple_of(s * 8, 8), 8)
    resp_copies = []
    for r in (1, 2, 3):
        resp_copies.append(remote(
            resp_ref.at[(s + r) % 4], response.at[:, rows_s, :],
            resp_send.at[r - 1], resp_recv.at[r - 1], in_group(r),
        ))
        resp_copies[-1].start()
    response[:, rows_s, :] = resp_ref[s]

    row = lax.broadcasted_iota(jnp.int32, (1024, 128), 0)
    lane = lax.broadcasted_iota(jnp.int32, (1024, 128), 1)
    for e in range(8):
        src = (lane // 16) % 2 * 512 + (lane // 32) * 128 + e * 16 + lane % 16
        perm[:, e * 128:(e + 1) * 128] = jnp.where(row == src, 1.0, 0.0).astype(BF16)

    all_tiles = ker_ref.at[pl.ds(0, 31)]
    pltpu.make_async_copy(all_tiles, all_tiles, ker_recv).wait()
    w_copies = []
    for r in (2, 1, 3):
        w_copies.append(remote(
            weights.at[y], weights.at[y], w_send.at[r - 1], w_recv.at[r - 1], along_y(r)
        ))
        w_copies[-1].start()

    other = (y * 4 + x_hi * 2 + 1 - core, inch)
    for copy in z_copies + zh_copies:
        copy.wait()
    x_copies = []
    for r in (2, 1, 3):
        view = pieces.at[x_hi, core, x_lo]
        x_copies.append(remote(view, view, x_send.at[r - 1], x_recv.at[r - 1], along_x(r)))
        x_copies[-1].start()
    c_copies = []
    for r in (0, 3, 1, 2):
        there = (x + 4 - r) % 4
        view = pieces.at[there // 2, core, there % 2]
        if r:
            x_copies[{2: 0, 1: 1, 3: 2}[r]].wait_recv()
        c_copies.append(remote(view, view, c_send.at[r], c_recv.at[r], other))
        c_copies[-1].start()
    for copy in c_copies:
        copy.wait_recv()

    at_start = y == 0
    halo = jnp.dot(
        jnp.concatenate([pieces[0, 0, 0, 256:288, :], pieces[0, 0, 1, 256:288, :]], axis=1),
        perm[...], preferred_element_type=F32,
    )
    halo = jnp.where(at_start, 0.0, halo)
    acc[0:128, 0:256] = jnp.concatenate(
        [halo[:, 256 * j:256 * (j + 1)] for j in range(4)], axis=0
    )
    for p1 in range(4):
        for e in range(8):
            for q in range(8):
                half = e % 2
                xe[p1 * 8 + e:p1 * 8 + e + 1, q * 128:(q + 1) * 128] = acc[
                    pl.ds((e // 2) * 32 + p1 * 8 + 7 - q, 1), half * 128:(half + 1) * 128
                ]
    first = lax.broadcasted_iota(jnp.int32, (256, 128), 0) % 32 == 0
    for p1 in range(4):
        stacked = jnp.concatenate(
            [
                jnp.concatenate(
                    [pieces[g // 2, g % 2, lo, p1 * 64:(p1 + 1) * 64, :] for lo in range(2)],
                    axis=1,
                )
                for g in range(4)
            ],
            axis=0,
        )
        for e in range(8):
            block = jnp.dot(
                stacked, perm[:, e * 128:(e + 1) * 128], preferred_element_type=F32
            )
            block = block.reshape(4, 8, 8, 128).transpose(1, 0, 2, 3).reshape(256, 128)
            edge = halo[p1 * 8:(p1 + 1) * 8, e * 128:(e + 1) * 128]
            edge = jnp.broadcast_to(edge[:, None, :], (8, 32, 128)).reshape(256, 128)
            before = jnp.where(first, edge, pltpu.roll(block, 1, axis=0))
            sb[p1 * 8 + e, 256:512, :] = block.astype(BF16)
            sb[p1 * 8 + e, 0:256, :] = before.astype(BF16)

    for copy in w_copies + resp_copies:
        copy.wait()

    wide_lane = lax.broadcasted_iota(jnp.int32, (256, 256), 1)
    wide_row = lax.broadcasted_iota(jnp.int32, (256, 256), 0)
    ext_lane = lax.broadcasted_iota(jnp.int32, (32, 256), 1)
    ext_row = lax.broadcasted_iota(jnp.int32, (32, 256), 0)

    def tap_matrix():
        return jnp.concatenate([weights[j] for j in range(4)], axis=0)

    def forward():
        acc[...] = jnp.zeros_like(acc)

        def group(g, carry):
            lhs = jnp.concatenate(
                [
                    jnp.concatenate(
                        [sb[g * 4 + j, (8 - q) * 32:(8 - q) * 32 + 256, :] for q in range(8)],
                        axis=1,
                    )
                    for j in range(4)
                ],
                axis=0,
            )
            product = jnp.dot(lhs, tap_matrix(), preferred_element_type=F32)
            here = acc[0:256, :]
            after = acc[256:512, :]
            for j in range(4):
                shift = (g * 4 + j) * 8
                turned = pltpu.roll(product[j * 256:(j + 1) * 256], shift, axis=1)
                keep = wide_lane >= shift
                here = here + jnp.where(keep, turned, 0.0)
                after = after + jnp.where(keep, 0.0, turned)
            acc[0:256, :] = here
            acc[256:512, :] = after
            return carry

        lax.fori_loop(0, 8, group, 0)
        edge = jnp.dot(xe[...].astype(BF16), tap_matrix(), preferred_element_type=F32)
        edge = pltpu.roll(edge, 0, axis=1, stride=8, stride_axis=0)
        edge = jnp.sum(jnp.where(ext_lane < ext_row * 8, edge, 0.0), axis=0, keepdims=True)
        after = acc[256:512, :]
        moved = jnp.where(
            wide_row >= 32, pltpu.roll(after, 32, axis=0), pltpu.roll(after, 33, axis=0)
        )
        moved = jnp.where(wide_row == 0, jnp.broadcast_to(edge, (256, 256)), moved)
        return (acc[0:256, :] + moved) * SCALE

    def expand(resid):
        later = jnp.where(
            wide_row < 224, pltpu.roll(resid, 224, axis=0), pltpu.roll(resid, 223, axis=0)
        )
        later = jnp.where(wide_row == 255, 0.0, later)
        here_t = resid.T
        later_t = later.T
        both = jnp.concatenate([here_t, later_t], axis=0)
        r_even[...] = both.astype(BF16)
        r_odd[...] = jnp.concatenate([both[8:], both[:8]], axis=0).astype(BF16)

    def edge_windows(resid):
        line = jnp.broadcast_to(resid[0:1, :], (32, 256))
        line = pltpu.roll(line, 8, axis=1, stride=8, stride_axis=0)
        return jnp.where(ext_lane + (31 - ext_row) * 8 >= 256, line, 0.0)

    def gradient_of(there, edges):
        total = jnp.zeros((256, 256), F32)
        top = pl.multiple_of((8 - 2 * there) * 32, 32)
        low = pl.multiple_of((7 - 2 * there) * 32, 32)
        for g in range(8):
            left = []
            right = []
            for p in range(4 * g, 4 * g + 4):
                windows = r_odd if p % 2 else r_even
                at = 8 * (p - p % 2)
                left.append(windows[at:at + 256, :])
                right.append(jnp.concatenate(
                    [sb[p, pl.ds(top, 256), :], sb[p, pl.ds(low, 256), :]], axis=1
                ))
            total = total + jnp.dot(
                jnp.concatenate(left, axis=1), jnp.concatenate(right, axis=0),
                preferred_element_type=F32,
            )
        lanes = pl.ds(pl.multiple_of(there * 256, 256), 256)
        total = total + jnp.dot(edges, xe[:, lanes].astype(BF16), preferred_element_type=F32)
        return total.T * SCALE

    def send_energy(turn):
        energy_own[turn, 0] = jnp.full((8, 128), jnp.sum(grad_own[...] * grad_own[...]), F32)

        def send(r, carry):
            remote(
                energy_own.at[turn, 0], energy_a.at[turn, r - 1],
                ea_send.at[turn], ea_recv.at[turn], in_plane((rank + r) % 32),
            ).start()
            return carry

        lax.fori_loop(1, 32, send, 0)

    def send_tiles(turn):

        def send(r, carry):
            d = (rank + r) % 32
            rows = pl.ds(pl.multiple_of(((d % 4) // 2) * 128 + (d // 4) * 16, 16), 16)
            lanes = pl.ds(pl.multiple_of((d % 2) * 128, 128), 128)
            remote(
                grad_all.at[turn, y, rows, lanes], tiles.at[turn, rank],
                t_send.at[turn], t_recv.at[turn], in_plane(d),
            ).start()
            return carry

        lax.fori_loop(1, 32, send, 0)
        tiles[turn, rank] = grad_all[turn, y, pl.ds(row_k, 16), pl.ds(lane_k, 128)]

    def finish_energy(turn):
        mine = energy_a.at[turn]
        pltpu.make_async_copy(mine, mine, ea_recv.at[turn]).wait()
        energy_own[turn, 1] = energy_own[turn, 0] + jnp.sum(energy_a[turn], axis=0)
        copies = []
        for r in (1, 2, 3):
            copies.append(remote(
                energy_own.at[turn, 1], energy_b.at[turn, r - 1],
                eb_send.at[turn, r - 1], eb_recv.at[turn, r - 1], along_y(r),
            ))
            copies[-1].start()
        for copy in copies:
            copy.wait_recv()
        total = energy_own[turn, 1] + jnp.sum(energy_b[turn], axis=0)
        factor = STEP_SIZE * lax.rsqrt(total / COUNT + EPSILON)
        return factor[0:1, :], copies

    factors = []
    pending = []
    for turn in range(2):
        predicted = forward()
        resid = (response[...].reshape(256, 256) - predicted).astype(BF16).astype(F32)
        if turn == 1:
            resid_all[...] = resid.reshape(8, 32, 256)
            for r in (1, 2, 3):
                there = pl.ds(pl.multiple_of(((s + r) % 4) * 8, 8), 8)
                pending.append(remote(
                    resid_all.at[:, there, :], resid_in.at[s],
                    o_send.at[r - 1], o_recv.at[r - 1], in_group(r),
                ))
                pending[-1].start()
        expand(resid)
        flipped = edge_windows(resid)
        edges = jnp.concatenate(
            [flipped[31 - j:32 - j, :] for j in range(32)], axis=0
        ).T.astype(BF16)
        rs_copies = []
        for r in (2, 1, 3):
            grad_out[r - 1] = gradient_of((y + r) % 4, edges).astype(BF16)
            rs_copies.append(remote(
                grad_out.at[r - 1], grad_in.at[r - 1],
                rs_send.at[turn, r - 1], rs_recv.at[turn, r - 1], along_y(r),
            ))
            rs_copies[-1].start()
        own = gradient_of(y, edges)
        for copy in rs_copies:
            copy.wait()
        for r in range(3):
            own = own + grad_in[r].astype(F32)
        grad_own[...] = own
        grad_all[turn, y] = own.astype(BF16)
        ag_copies = []
        if turn == 0:
            for r in (2, 1, 3):
                ag_copies.append(remote(
                    grad_all.at[turn, y], grad_all.at[turn, y],
                    ag_send.at[r - 1], ag_recv.at[r - 1], along_y(r),
                ))
                ag_copies[-1].start()
        send_energy(turn)
        send_tiles(turn)
        factor, copies = finish_energy(turn)
        factors.append(factor)
        pending += [("send", copy) for copy in copies]
        if turn == 0:
            for copy in ag_copies:
                copy.wait()
            wide = jnp.concatenate([factor, factor], axis=1)
            for j in range(4):
                weights[j] = (
                    weights[j].astype(F32) + wide * grad_all[0, j].astype(F32)
                ).astype(BF16)

    for turn in range(2):
        half = tiles.at[turn, pl.ds(0, 31)]
        pltpu.make_async_copy(half, half, t_recv.at[turn]).wait()
    step_ref[...] = (
        factors[0] * tiles[0].astype(F32) + factors[1] * tiles[1].astype(F32)
    )
    for item in pending:
        if isinstance(item, tuple):
            item[1].wait_send()
        else:
            item.wait()
    resid_ref[...] = resid_in[...]
    resid_ref[s] = resid_all[:, rows_s, :]

    pltpu.make_async_copy(all_tiles, all_tiles, ker_send).wait()
    for copy in x_copies + c_copies:
        copy.wait_send()
    for turn in range(2):
        mine = energy_a.at[turn]
        pltpu.make_async_copy(mine, mine, ea_send.at[turn]).wait()
        half = tiles.at[turn, pl.ds(0, 31)]
        pltpu.make_async_copy(half, half, t_send.at[turn]).wait()


def local(signal, response, kernel):
    inch = lax.axis_index("inch")
    sig = signal.reshape(8, 8, 4, 8, 16).transpose(2, 1, 0, 3, 4)
    tail = sig[:, :, 7].reshape(32, 128)
    sig = sig.reshape(256, 128)
    ker = kernel.astype(BF16).reshape(16, 16, 32, 8).transpose(2, 1, 0, 3).reshape(32, 16, 128)
    resp = lax.dynamic_slice_in_dim(response, inch * 32, 32, 1).astype(F32)
    resp = resp.reshape(8, 8, 32, 4, 8).transpose(3, 1, 0, 2, 4).reshape(4, 8, 8, 256)
    dma = pltpu.SemaphoreType.DMA
    vmem = pl.BlockSpec(memory_space=pltpu.VMEM)
    step, resid = pl.pallas_call(
        body,
        out_shape=(
            jax.ShapeDtypeStruct((32, 16, 128), F32),
            jax.ShapeDtypeStruct((4, 8, 8, 256), F32),
        ),
        in_specs=[vmem] * 4,
        out_specs=(vmem, vmem),
        scratch_shapes=[
            pltpu.VMEM((2, 2, 2, 288, 512), BF16),
            pltpu.VMEM((32, 128), BF16),
            pltpu.VMEM((1024, 1024), BF16),
            pltpu.VMEM((32, 512, 128), BF16),
            pltpu.VMEM((32, 1024), F32),
            pltpu.VMEM((4, 256, 256), BF16),
            pltpu.VMEM((8, 32, 256), F32),
            pltpu.VMEM((512, 256), BF16),
            pltpu.VMEM((512, 256), BF16),
            pltpu.VMEM((3, 256, 256), BF16),
            pltpu.VMEM((3, 256, 256), BF16),
            pltpu.VMEM((256, 256), F32),
            pltpu.VMEM((2, 4, 256, 256), BF16),
            pltpu.VMEM((2, 32, 16, 128), BF16),
            pltpu.VMEM((2, 31, 8, 128), F32),
            pltpu.VMEM((2, 3, 8, 128), F32),
            pltpu.VMEM((2, 2, 8, 128), F32),
            pltpu.VMEM((512, 256), F32),
            pltpu.VMEM((8, 32, 256), F32),
            pltpu.VMEM((4, 8, 8, 256), F32),
            dma, dma, dma((3,)), dma((3,)), dma, dma,
            dma((3,)), dma((3,)), dma((3,)), dma((3,)), dma((3,)), dma((3,)), dma((4,)), dma((4,)),
            dma((3,)), dma((3,)), dma((2, 3)), dma((2, 3)), dma((3,)), dma((3,)),
            dma((2,)), dma((2,)), dma((2, 3)), dma((2, 3)), dma((2,)), dma((2,)), dma((3,)), dma((3,)),
        ],
        compiler_params=pltpu.CompilerParams(
            collective_id=0, has_side_effects=True, vmem_limit_bytes=60 * 2**20
        ),
    )(sig, tail, ker, resp)
    kernel_out = kernel + step.reshape(32, 16, 16, 8).transpose(2, 1, 0, 3).reshape(16, 16, 256)
    resid = resid.astype(BF16).reshape(4, 8, 8, 32, 8).transpose(2, 1, 3, 0, 4).reshape(2048, 32)
    return kernel_out, resid


def solution(mesh):
    placed = (P("tm", "inch"), P("tm", None), P("tm", "inch", None))
    return jax.shard_map(
        local,
        mesh=mesh,
        in_specs=placed,
        out_specs=(P("tm", "inch", None), P("tm", "inch")),
        check_vma=False,
    )
```

profile of v0, /device:TPU:1, one launch (start us, length us, event | category | flops | bytes accessed | tf_op | source)
XLA Modules:
  0.0 129.9 jit_solution(15672205436246525660)
XLA Ops:
  0.6 0.0 copy-start
  0.6 1.2 copy-done
  1.9 0.2 constant_dynamic-slice_fusion
  2.1 0.2 copy.49
  2.3 0.4 reshape.52
  2.6 2.7 %copy.42 = f32[4,8,8,32,8]{4,3,2,1,0:T(8,128)} copy(f32[4,8,8,32,8]{3,1,2,4,0:T(8,128)S(1)} %bitcast.32) | data formatting | bytes 524288 | tf_op jit(solution)/shard_map/reshape | solution.py:418
  5.3 0.0 copy-start.3
  5.3 4.7 %reshape.49.resp_ref = f32[4,8,8,256]{3,2,1,0:T(8,128)} reshape(f32[4,8,8,32,8]{4,3,2,1,0:T(8,128)} %copy.42) | data formatting | bytes 524288 | tf_op jit(solution)/shard_map/reshape | solution.py:418
  10.0 0.0 copy-done.3
  10.0 0.0 copy-start.1
  10.0 0.3 copy.36
  10.3 0.1 copy.37
  10.4 1.0 reshape.38.sig_ref
  11.4 0.7 reshape_squeeze.3.tail_ref
  12.1 0.0 copy-done.1
  12.2 0.5 copy.39
  12.6 1.2 copy.40
  13.9 0.9 copy.43.ker_ref
  14.8 96.1 %shard_map.50 = (f32[32,16,128]{2,1,0:T(8,128)}, f32[4,8,8,256]{3,2,1,0:T(8,128)}) custom-call(bf16[256,128]{1,0:T(8,128)(2,1)} %reshape.38.sig_ref, bf16[32,128]{1,0:T(8,128)(2,1)} %reshape_squeeze.3.tail_ref, bf16[32,16,128]{2,1,0:T(8,128)(2,1)} %copy.43.ker_ref, f32[4,8,8,256]{3,2,1,0:T(8,128)} %reshape.49.resp_ref), custom_call_target="tpu_custom_call" | custom-call | tf_op jit(solution)/shard_map/pallas_call | solution.py:421
  110.9 2.3 %copy.44 = f32[32,16,128]{0,2,1:T(8,128)} copy(f32[32,16,128]{2,1,0:T(8,128)} %get-tuple-element.4) | data formatting | bytes 524288 | tf_op jit(solution)/shard_map/pallas_call | solution.py:421
  113.1 2.1 %copy.45 = f32[16,16,32,8]{1,3,2,0:T(8,128)S(1)} copy(f32[16,16,32,8]{2,3,0,1:T(8,128)} %bitcast.31) | data formatting | bytes 524288 | tf_op jit(solution)/shard_map/transpose | solution.py:459
  115.2 1.9 %copy.46 = f32[16,16,256]{1,2,0:T(8,128)} copy(f32[16,16,256]{2,1,0:T(8,128)S(1)} %copy-done.1) | data formatting | bytes 524288 | tf_op args[2]
  117.1 3.1 %bitcast_add_fusion = f32[16,16,256]{1,2,0:T(8,128)} fusion(f32[16,16,256]{1,2,0:T(8,128)} %copy.46, f32[16,16,32,8]{1,3,2,0:T(8,128)S(1)} %copy.45), kind=kLoop, calls=%fused_computation | loop fusion | flops 65536 | bytes 786432 | tf_op jit(solution)/shard_map/add | solution.py:459
  120.2 0.0 copy-start.2
  120.3 2.9 %copy.48 = f32[16,16,256]{2,1,0:T(8,128)} copy(f32[16,16,256]{1,2,0:T(8,128)} %bitcast_add_fusion) | data formatting | bytes 524288
  123.2 0.0 copy-done.2
  123.2 2.5 %reshape.46 = bf16[4,8,8,32,8]{4,3,2,1,0:T(8,128)(2,1)S(1)} reshape(bf16[4,8,8,256]{3,2,1,0:T(8,128)(2,1)S(1)} %convert_element_type.8) | data formatting | bytes 262144 | tf_op jit(solution)/shard_map/reshape | solution.py:460
  125.7 1.9 %copy.47 = bf16[8,8,32,4,8]{2,1,0,4,3:T(8,128)(2,1)} copy(bf16[8,8,32,4,8]{4,2,0,1,3:T(8,128)(2,1)S(1)} %bitcast.30) | data formatting | bytes 262144 | tf_op jit(solution)/shard_map/transpose | solution.py:460
  127.6 2.3 %reshape.47 = bf16[2048,32]{0,1:T(8,128)(2,1)} reshape(bf16[8,8,32,4,8]{2,1,0,4,3:T(8,128)(2,1)} %copy.47) | data formatting | bytes 262144 | tf_op jit(solution)/shard_map/reshape | solution.py:460
  (4 shorter events, 0.1 us)
Async XLA Ops:
  0.6 1.2 copy-start
  5.3 4.7 %copy-start.3 = (bf16[2048,16]{0,1:T(8,128)(2,1)S(1)}, bf16[2048,16]{0,1:T(8,128)(2,1)}, u32[]{:S(2)}) copy-start(bf16[2048,16]{0,1:T(8,128)(2,1)} %param.3) | copy-start | bytes 196612
  10.0 2.1 %copy-start.1 = (f32[16,16,256]{2,1,0:T(8,128)S(1)}, f32[16,16,256]{2,1,0:T(8,128)}, u32[]{:S(2)}) copy-start(f32[16,16,256]{2,1,0:T(8,128)} %param.5) | copy-start | bytes 786436
  120.2 2.9 %copy-start.2 = (f32[4,8,8,256]{3,2,1,0:T(8,128)S(1)}, f32[4,8,8,256]{3,2,1,0:T(8,128)}, u32[]{:S(2)}) copy-start(f32[4,8,8,256]{3,2,1,0:T(8,128)} %get-tuple-element.5) | copy-start | bytes 786436
where the time goes:
time: 130 us
  Pallas kernels  96.1 us (74%)
  local copies, waits for them, and re-layouts  29.9 us (23%)
  other arithmetic  3.17 us (2%)
    pallas_call x1, Pallas kernels, local(): pl.pallas_call(body, out_shape=(jax.ShapeDtypeStruct((32, 16, 128), F32),...  96.1 us
    reshape x3, local copies, waits for them, and re-layouts, local(): resp.reshape(8, 8, 32, 4, 8).transpose(3, 1, 0, 2, 4).reshape(4, 8, 8, 256)  7.75 us
    unnamed x12, local copies, waits for them, and re-layouts  6.54 us
    reshape x2, local copies, waits for them, and re-layouts, local(): resid.astype(BF16).reshape(4, 8, 8, 32, 8).transpose(2, 1, 3, 0, 4)  4.76 us
    add x1, other arithmetic, local(): kernel + step.reshape(32, 16, 16, 8).transpose(2, 1, 0, 3).reshape(16, 16...  3.14 us

commit v1 on v0

v1 whole, which is shorter than its diff:
```python
import math

import jax
import jax.numpy as jnp
from jax import lax
from jax.experimental import pallas as pl
from jax.experimental.pallas import tpu as pltpu
from jax.sharding import PartitionSpec as P

STEP_SIZE = 0.5
EPSILON = 1e-06
F32 = jnp.float32
BF16 = jnp.bfloat16
MESH = pl.DeviceIdType.MESH
TAPS = 256
CI = 128
CO = 256
SCALE = 1.0 / math.sqrt(TAPS * CI)
COUNT = TAPS * CI * CO


def remote(src, dst, send, recv, device):
    return pltpu.make_async_remote_copy(
        src_ref=src, dst_ref=dst, send_sem=send, recv_sem=recv,
        device_id=device, device_id_type=MESH,
    )


def swap_blocks(parts):
    parts = list(parts)
    for bit in (1, 2, 4, 8):
        parts = swap_stage(parts, bit)
    return parts


def swap_stage(parts, bit):
    lane = lax.broadcasted_iota(jnp.int32, parts[0].shape, 1)
    high = (lane & (8 * bit)) != 0
    result = list(parts)
    for i in range(len(parts)):
        if not i & bit:
            low_part, high_part = parts[i], parts[i | bit]
            result[i] = jnp.where(high, pltpu.roll(high_part, 8 * bit, axis=1), low_part)
            result[i | bit] = jnp.where(
                high, high_part, pltpu.roll(low_part, 128 - 8 * bit, axis=1)
            )
    return result


def body(
    sig_ref, resp_hbm, ker_ref,
    kernel_ref, resid_ref,
    gathered, rows, ker_tiles, resp_raw, resp_wide, resp_out, resid_wide, base,
    sb, xe, weights, response, r_even, r_odd,
    grad_out, grad_in, grad_own, grad_all, tiles, energy_a, energy_b, energy_own, acc, resid_all,
    resid_in,
    hbm_sem, ker_send, ker_recv, resp_send, resp_recv, tail_send, tail_recv,
    za_send, za_recv, zh_send, zh_recv, xb_send, xb_recv, xa_send, xa_recv,
    zb_send, zb_recv, ca_send, ca_recv, cb_send, cb_recv,
    w_send, w_recv, rs_send, rs_recv, ag_send, ag_recv,
    ea_send, ea_recv, eb_send, eb_recv, t_send, t_recv, o_send, o_recv,
):
    tm = lax.axis_index("tm")
    inch = lax.axis_index("inch")
    y = tm // 4
    s = tm % 4
    x_hi = s // 2
    core = s % 2
    z = inch // 2
    x_lo = inch % 2
    x = x_hi * 2 + x_lo
    rank = inch * 4 + s

    def in_plane(d):
        return (y * 4 + d % 4, d // 4)

    def along_y(r):
        return ((((y + r) % 4) * 4) + s, inch)

    def along_z(r):
        return (tm, ((z + r) % 4) * 2 + x_lo)

    def along_x(r):
        there = (x + r) % 4
        return (y * 4 + (there // 2) * 2 + core, z * 2 + there % 2)

    def in_group(r):
        return (y * 4 + (s + r) % 4, inch)

    barrier = pltpu.get_barrier_semaphore()

    def greet(r, carry):
        pl.semaphore_signal(
            barrier, inc=1, device_id=in_plane((rank + r) % 32), device_id_type=MESH
        )
        return carry

    lax.fori_loop(1, 32, greet, 0)
    for r in (1, 2, 3):
        pl.semaphore_signal(barrier, inc=1, device_id=along_y(r), device_id_type=MESH)
    pl.semaphore_signal(
        barrier, inc=1, device_id=((tm + 15) % 16, inch), device_id_type=MESH
    )

    columns = pl.ds(pl.multiple_of((inch // 4) * 128, 128), 128)
    fetch = pltpu.make_async_copy(resp_hbm.at[:, columns], resp_raw, hbm_sem)
    fetch.start()
    row_z = pl.ds(pl.multiple_of(z * 16, 16), 16)
    gathered[x_hi, core, x_lo, row_z, 256:2304] = sig_ref[...]
    part_h, part_a, part_b = pl.ds(0, 256), pl.ds(256, 1024), pl.ds(1280, 1024)
    part_ha = pl.ds(0, 1280)

    pl.semaphore_wait(barrier, 35)

    nxt = (tm + 1) % 16
    tail_copy = remote(
        sig_ref.at[:, pl.ds(1792, 256)],
        gathered.at[(nxt % 4) // 2, nxt % 2, x_lo, row_z, part_h],
        tail_send, tail_recv, (nxt, inch),
    )
    tail_copy.start()
    za_copies = []
    xb_copies = []
    for r in (2, 1, 3):
        view = gathered.at[x_hi, core, x_lo, row_z, part_a]
        za_copies.append(remote(view, view, za_send.at[r - 1], za_recv.at[r - 1], along_z(r)))
        za_copies[-1].start()
        view = gathered.at[x_hi, core, x_lo, row_z, part_b]
        xb_copies.append(remote(view, view, xb_send.at[r - 1], xb_recv.at[r - 1], along_x(r)))
        xb_copies[-1].start()

    for half in range(2):
        swapped = swap_blocks([ker_ref[u, :, half * 128:(half + 1) * 128] for u in range(16)])
        for d in range(16):
            ker_tiles[half * 16 + d] = swapped[d].astype(BF16)
    row_k = pl.multiple_of((s // 2) * 128 + x_lo * 64 + z * 16, 16)
    lane_k = pl.multiple_of((s % 2) * 128, 128)

    def send_taps(r, carry):
        d = (rank + r) % 32
        remote(
            ker_tiles.at[d], weights.at[y, pl.ds(row_k, 16), pl.ds(lane_k, 128)],
            ker_send, ker_recv, in_plane(d),
        ).start()
        return carry

    lax.fori_loop(1, 32, send_taps, 0)
    weights[y, pl.ds(row_k, 16), pl.ds(lane_k, 128)] = ker_tiles[rank]

    tail_copy.wait()
    zh_copies = []
    for r in (2, 1, 3):
        view = gathered.at[x_hi, core, x_lo, row_z, part_h]
        zh_copies.append(remote(view, view, zh_send.at[r - 1], zh_recv.at[r - 1], along_z(r)))
        zh_copies[-1].start()

    other = (y * 4 + x_hi * 2 + 1 - core, inch)
    zb_copies = {}

    def pass_b(r):
        there = (x + 4 - r) % 4
        for k in (2, 1, 3):
            view = gathered.at[there // 2, core, there % 2, row_z, part_b]
            copy = remote(view, view, zb_send.at[r, k - 1], zb_recv.at[r, k - 1], along_z(k))
            copy.start()
            zb_copies[r, k] = copy

    place = {2: 0, 1: 1, 3: 2}
    pass_b(0)
    for copy in za_copies + zh_copies:
        copy.wait_recv()
    xa_copies = []
    for r in (2, 1, 3):
        view = gathered.at[x_hi, core, x_lo, :, part_ha]
        xa_copies.append(remote(view, view, xa_send.at[r - 1], xa_recv.at[r - 1], along_x(r)))
        xa_copies[-1].start()
    for r in (1, 3, 2):
        xb_copies[place[r]].wait_recv()
        pass_b(r)

    all_tiles = ker_tiles.at[pl.ds(0, 31)]
    pltpu.make_async_copy(all_tiles, all_tiles, ker_recv).wait()
    w_copies = []
    for r in (2, 1, 3):
        w_copies.append(remote(
            weights.at[y], weights.at[y], w_send.at[r - 1], w_recv.at[r - 1], along_y(r)
        ))
        w_copies[-1].start()

    fetch.wait()
    turn_by = (128 - (inch % 4) * 32) % 128

    def widen(k, carry):
        at = pl.ds(pl.multiple_of(k * 256, 256), 256)
        resp_wide[at, :] = pltpu.roll(resp_raw[at, :].astype(F32), turn_by, axis=1)
        return carry

    lax.fori_loop(0, 8, widen, 0)

    def merge(parts, bit):
        lane = lax.broadcasted_iota(jnp.int32, parts[0].shape, 1)
        high = (lane & (8 * bit)) != 0
        return [
            jnp.where(high, pltpu.roll(parts[i | bit], 8 * bit, axis=1), parts[i])
            for i in range(len(parts)) if not i & bit
        ]

    def pack_response(b, carry):
        for half in range(2):
            parts = [
                resp_wide[pl.ds(b * 32 + half * 16 + p, 8, stride=256), :] for p in range(16)
            ]
            parts = merge(merge(parts, 8), 4)
            parts = swap_stage(swap_stage(parts, 1), 2)
            for g in range(4):
                resp_out[g, b, :, half * 128:(half + 1) * 128] = parts[g]
        return carry

    lax.fori_loop(0, 8, pack_response, 0)
    rows_s = pl.ds(pl.multiple_of(s * 8, 8), 8)
    resp_copies = []
    for r in (1, 2, 3):
        resp_copies.append(remote(
            resp_out.at[(s + r) % 4], response.at[:, rows_s, :],
            resp_send.at[r - 1], resp_recv.at[r - 1], in_group(r),
        ))
        resp_copies[-1].start()
    response[:, rows_s, :] = resp_out[s]

    ca_copies = []
    cb_copies = []
    for r in (0, 1, 3, 2):
        there = (x + 4 - r) % 4
        if r:
            xa_copies[place[r]].wait_recv()
        view = gathered.at[there // 2, core, there % 2, :, part_ha]
        ca_copies.append(remote(view, view, ca_send.at[r], ca_recv.at[r], other))
        ca_copies[-1].start()
        for k in (1, 2, 3):
            zb_copies[r, k].wait_recv()
        view = gathered.at[there // 2, core, there % 2, :, part_b]
        cb_copies.append(remote(view, view, cb_send.at[r], cb_recv.at[r], other))
        cb_copies[-1].start()

    def upright(hi, of_core):
        def one(k, carry):
            lanes = pl.ds(pl.multiple_of(256 + k * 128, 128), 128)
            block = jnp.concatenate(
                [gathered[hi, of_core, 0, :, lanes], gathered[hi, of_core, 1, :, lanes]], axis=0
            )
            at = pl.multiple_of(256 + (hi * 2 + of_core) * 2048 + k * 128, 128)
            rows[pl.ds(at, 128), :] = block.astype(F32).T
            return carry

        lax.fori_loop(0, 16, one, 0)

    for hi in range(2):
        upright(hi, core)
    for copy in ca_copies + cb_copies:
        copy.wait_recv()
    for hi in range(2):
        upright(hi, 1 - core)
    at_start = y == 0
    for k in range(2):
        block = jnp.concatenate(
            [gathered[0, 0, lo, :, k * 128:(k + 1) * 128] for lo in range(2)], axis=0
        )
        rows[k * 128:(k + 1) * 128, :] = jnp.where(at_start, 0.0, block.astype(F32).T)
    for q in range(8):
        xe[:, q * 128:(q + 1) * 128] = rows[(7 - q) * 32:(8 - q) * 32, :].astype(BF16)

    def order(p, carry):
        for b in range(8):
            sb[p, b * 32:(b + 1) * 32, :] = rows[
                pl.ds(b * 32 + p, 32, stride=256), :
            ].astype(BF16)
            sb[p, 256 + b * 32:256 + (b + 1) * 32, :] = rows[
                pl.ds(256 + b * 32 + p, 32, stride=256), :
            ].astype(BF16)
        return carry

    lax.fori_loop(0, 32, order, 0)

    for copy in w_copies + resp_copies:
        copy.wait()

    wide_lane = lax.broadcasted_iota(jnp.int32, (256, 256), 1)
    wide_row = lax.broadcasted_iota(jnp.int32, (256, 256), 0)
    ext_lane = lax.broadcasted_iota(jnp.int32, (32, 256), 1)
    ext_row = lax.broadcasted_iota(jnp.int32, (32, 256), 0)

    def forward(taps):
        def tap_matrix():
            return jnp.concatenate([taps[j] for j in range(4)], axis=0)

        acc[...] = jnp.zeros_like(acc)

        def group(g, carry):
            lhs = jnp.concatenate(
                [
                    jnp.concatenate(
                        [sb[g * 4 + j, (8 - q) * 32:(8 - q) * 32 + 256, :] for q in range(8)],
                        axis=1,
                    )
                    for j in range(4)
                ],
                axis=0,
            )
            product = jnp.dot(lhs, tap_matrix(), preferred_element_type=F32)
            here = acc[0:256, :]
            after = acc[256:512, :]
            for j in range(4):
                shift = (g * 4 + j) * 8
                turned = pltpu.roll(product[j * 256:(j + 1) * 256], shift, axis=1)
                keep = wide_lane >= shift
                here = here + jnp.where(keep, turned, 0.0)
                after = after + jnp.where(keep, 0.0, turned)
            acc[0:256, :] = here
            acc[256:512, :] = after
            return carry

        lax.fori_loop(0, 8, group, 0)
        edge = jnp.dot(xe[...], tap_matrix(), preferred_element_type=F32)
        edge = pltpu.roll(edge, 0, axis=1, stride=8, stride_axis=0)
        edge = jnp.sum(jnp.where(ext_lane < ext_row * 8, edge, 0.0), axis=0, keepdims=True)
        after = acc[256:512, :]
        moved = jnp.where(
            wide_row >= 32, pltpu.roll(after, 32, axis=0), pltpu.roll(after, 33, axis=0)
        )
        moved = jnp.where(wide_row == 0, jnp.broadcast_to(edge, (256, 256)), moved)
        return (acc[0:256, :] + moved) * SCALE

    def expand(resid):
        later = jnp.where(
            wide_row < 224, pltpu.roll(resid, 224, axis=0), pltpu.roll(resid, 223, axis=0)
        )
        later = jnp.where(wide_row == 255, 0.0, later)
        here_t = resid.T
        later_t = later.T
        both = jnp.concatenate([here_t, later_t], axis=0)
        r_even[...] = both.astype(BF16)
        r_odd[...] = jnp.concatenate([both[8:], both[:8]], axis=0).astype(BF16)

    def edge_windows(resid):
        line = jnp.broadcast_to(resid[0:1, :], (32, 256))
        line = pltpu.roll(line, 8, axis=1, stride=8, stride_axis=0)
        return jnp.where(ext_lane + (31 - ext_row) * 8 >= 256, line, 0.0)

    def gradient_of(there, edges):
        total = jnp.zeros((256, 256), F32)
        top = pl.multiple_of((8 - 2 * there) * 32, 32)
        low = pl.multiple_of((7 - 2 * there) * 32, 32)
        for g in range(8):
            left = []
            right = []
            for p in range(4 * g, 4 * g + 4):
                windows = r_odd if p % 2 else r_even
                at = 8 * (p - p % 2)
                left.append(windows[at:at + 256, :])
                right.append(jnp.concatenate(
                    [sb[p, pl.ds(top, 256), :], sb[p, pl.ds(low, 256), :]], axis=1
                ))
            total = total + jnp.dot(
                jnp.concatenate(left, axis=1), jnp.concatenate(right, axis=0),
                preferred_element_type=F32,
            )
        lanes = pl.ds(pl.multiple_of(there * 256, 256), 256)
        total = total + jnp.dot(edges, xe[:, lanes], preferred_element_type=F32)
        return total.T * SCALE

    def send_energy(turn):
        energy_own[turn, 0] = jnp.full((8, 128), jnp.sum(grad_own[...] * grad_own[...]), F32)

        def send(r, carry):
            remote(
                energy_own.at[turn, 0], energy_a.at[turn, r - 1],
                ea_send.at[turn], ea_recv.at[turn], in_plane((rank + r) % 32),
            ).start()
            return carry

        lax.fori_loop(1, 32, send, 0)

    def send_tiles(turn):

        def send(r, carry):
            d = (rank + r) % 32
            to = d // 4
            rows_d = pl.multiple_of(((d % 4) // 2) * 128 + (to % 2) * 64 + (to // 2) * 16, 16)
            lanes = pl.ds(pl.multiple_of((d % 2) * 128, 128), 128)
            remote(
                grad_all.at[turn, y, pl.ds(rows_d, 16), lanes], tiles.at[turn, rank],
                t_send.at[turn], t_recv.at[turn], in_plane(d),
            ).start()
            return carry

        lax.fori_loop(1, 32, send, 0)
        tiles[turn, rank] = grad_all[turn, y, pl.ds(row_k, 16), pl.ds(lane_k, 128)]

    def pass_energy(turn):
        mine = energy_a.at[turn]
        pltpu.make_async_copy(mine, mine, ea_recv.at[turn]).wait()
        energy_own[turn, 1] = energy_own[turn, 0] + jnp.sum(energy_a[turn], axis=0)
        copies = []
        for r in (1, 2, 3):
            copies.append(remote(
                energy_own.at[turn, 1], energy_b.at[turn, r - 1],
                eb_send.at[turn, r - 1], eb_recv.at[turn, r - 1], along_y(r),
            ))
            copies[-1].start()
        return copies

    def finish_energy(turn, copies):
        for copy in copies:
            copy.wait()
        total = energy_own[turn, 1] + jnp.sum(energy_b[turn], axis=0)
        factor = STEP_SIZE * lax.rsqrt(total / COUNT + EPSILON)
        return factor[0:1, :]

    factors = []
    resid_copies = []
    energy_copies = None
    for turn in range(2):
        if turn == 0:
            predicted = forward(weights)
            base[...] = predicted
        else:
            change = forward(grad_all.at[0])
            factors.append(finish_energy(0, energy_copies))
            wide = jnp.concatenate([factors[0], factors[0]], axis=1)
            predicted = base[...] + wide * change
        resid = (response[...].reshape(256, 256) - predicted).astype(BF16).astype(F32)
        if turn == 1:
            resid_all[...] = resid.reshape(8, 32, 256)
            for r in (1, 2, 3):
                there = pl.ds(pl.multiple_of(((s + r) % 4) * 8, 8), 8)
                resid_copies.append(remote(
                    resid_all.at[:, there, :], resid_in.at[s],
                    o_send.at[r - 1], o_recv.at[r - 1], in_group(r),
                ))
                resid_copies[-1].start()
            resid_in[s] = resid_all[:, rows_s, :]
        expand(resid)
        flipped = edge_windows(resid)
        edges = jnp.concatenate(
            [flipped[31 - j:32 - j, :] for j in range(32)], axis=0
        ).T.astype(BF16)
        rs_copies = []
        for r in (2, 1, 3):
            grad_out[r - 1] = gradient_of((y + r) % 4, edges).astype(BF16)
            rs_copies.append(remote(
                grad_out.at[r - 1], grad_in.at[r - 1],
                rs_send.at[turn, r - 1], rs_recv.at[turn, r - 1], along_y(r),
            ))
            rs_copies[-1].start()
        own = gradient_of(y, edges)
        for copy in rs_copies:
            copy.wait()
        for r in range(3):
            own = own + grad_in[r].astype(F32)
        grad_own[...] = own
        grad_all[turn, y] = own.astype(BF16)
        ag_copies = []
        if turn == 0:
            for r in (2, 1, 3):
                ag_copies.append(remote(
                    grad_all.at[turn, y], grad_all.at[turn, y],
                    ag_send.at[r - 1], ag_recv.at[r - 1], along_y(r),
                ))
                ag_copies[-1].start()
        send_energy(turn)
        send_tiles(turn)
        energy_copies = pass_energy(turn)
        for copy in ag_copies:
            copy.wait()

    for copy in resid_copies:
        copy.wait()

    def unpack_residual(b, carry):
        for half in range(2):
            parts = [resid_in[g, b, :, half * 128:(half + 1) * 128] for g in range(4)]
            parts = swap_stage(swap_stage(parts, 1), 2)
            for m in range(4):
                for l in range(4):
                    part = parts[l] if m == 0 else pltpu.roll(parts[l], 128 - 32 * m, axis=1)
                    at = b * 32 + half * 16 + 4 * m + l
                    resid_wide[pl.ds(at, 8, stride=256), :] = part
        return carry

    lax.fori_loop(0, 8, unpack_residual, 0)
    for k in range(16):
        flat = resid_wide[k * 128:(k + 1) * 128, :].T
        resid_ref[:, k * 128:(k + 1) * 128] = flat[0:32, :].astype(BF16)

    factors.append(finish_energy(1, energy_copies))
    for turn in range(2):
        half = tiles.at[turn, pl.ds(0, 31)]
        pltpu.make_async_copy(half, half, t_recv.at[turn]).wait()
    for half in range(2):
        steps = [
            factors[0] * tiles[0, half * 16 + d].astype(F32)
            + factors[1] * tiles[1, half * 16 + d].astype(F32)
            for d in range(16)
        ]
        lanes = slice(half * 128, (half + 1) * 128)
        for u, step in enumerate(swap_blocks(steps)):
            kernel_ref[u, :, lanes] = ker_ref[u, :, lanes] + step

    pltpu.make_async_copy(all_tiles, all_tiles, ker_send).wait()
    for copy in za_copies + zh_copies + xb_copies + xa_copies + ca_copies + cb_copies:
        copy.wait_send()
    for copy in zb_copies.values():
        copy.wait_send()
    for turn in range(2):
        mine = energy_a.at[turn]
        pltpu.make_async_copy(mine, mine, ea_send.at[turn]).wait()
        half = tiles.at[turn, pl.ds(0, 31)]
        pltpu.make_async_copy(half, half, t_send.at[turn]).wait()


def local(signal, response, kernel):
    dma = pltpu.SemaphoreType.DMA
    vmem = pl.BlockSpec(memory_space=pltpu.VMEM)
    kernel_out, resid = pl.pallas_call(
        body,
        out_shape=(
            jax.ShapeDtypeStruct((16, 16, 256), F32),
            jax.ShapeDtypeStruct((32, 2048), BF16),
        ),
        in_specs=[vmem, pl.BlockSpec(memory_space=pl.ANY), vmem],
        out_specs=(vmem, vmem),
        scratch_shapes=[
            pltpu.VMEM((2, 2, 2, 64, 2304), BF16),
            pltpu.VMEM((8448, 128), F32),
            pltpu.VMEM((32, 16, 128), BF16),
            pltpu.VMEM((2048, 128), BF16),
            pltpu.VMEM((2048, 128), F32),
            pltpu.VMEM((4, 8, 8, 256), F32),
            pltpu.VMEM((2048, 128), F32),
            pltpu.VMEM((256, 256), F32),
            pltpu.VMEM((32, 512, 128), BF16),
            pltpu.VMEM((32, 1024), BF16),
            pltpu.VMEM((4, 256, 256), BF16),
            pltpu.VMEM((8, 32, 256), F32),
            pltpu.VMEM((512, 256), BF16),
            pltpu.VMEM((512, 256), BF16),
            pltpu.VMEM((3, 256, 256), BF16),
            pltpu.VMEM((3, 256, 256), BF16),
            pltpu.VMEM((256, 256), F32),
            pltpu.VMEM((2, 4, 256, 256), BF16),
            pltpu.VMEM((2, 32, 16, 128), BF16),
            pltpu.VMEM((2, 31, 8, 128), F32),
            pltpu.VMEM((2, 3, 8, 128), F32),
            pltpu.VMEM((2, 2, 8, 128), F32),
            pltpu.VMEM((512, 256), F32),
            pltpu.VMEM((8, 32, 256), F32),
            pltpu.VMEM((4, 8, 8, 256), F32),
            dma, dma, dma, dma((3,)), dma((3,)), dma, dma,
            dma((3,)), dma((3,)), dma((3,)), dma((3,)), dma((3,)), dma((3,)), dma((3,)), dma((3,)),
            dma((4, 3)), dma((4, 3)), dma((4,)), dma((4,)), dma((4,)), dma((4,)),
            dma((3,)), dma((3,)), dma((2, 3)), dma((2, 3)), dma((3,)), dma((3,)),
            dma((2,)), dma((2,)), dma((2, 3)), dma((2, 3)), dma((2,)), dma((2,)), dma((3,)), dma((3,)),
        ],
        compiler_params=pltpu.CompilerParams(
            collective_id=0, has_side_effects=True, vmem_limit_bytes=60 * 2**20
        ),
    )(signal.T, response, kernel)
    return kernel_out, resid.T


def solution(mesh):
    placed = (P("tm", "inch"), P("tm", None), P("tm", "inch", None))
    return jax.shard_map(
        local,
        mesh=mesh,
        in_specs=placed,
        out_specs=(P("tm", "inch", None), P("tm", "inch")),
        check_vma=False,
    )
```

time: 130 us -> 97 us (0.75)
  local copies, waits for them, and re-layouts: 29.9 us -> 2.37 us
  other arithmetic: 3.17 us -> 0 us
  Pallas kernels: 96.1 us -> 93.9 us
    reshape x7 -> x0, local copies, waits for them, and re-layouts: 14.4 us -> none  [the longest x3 7.75 us: local(): resp.reshape(8, 8, 32, 4, 8).transpose(3, 1, 0, 2, 4).reshape(4, 8, 8, 256)]
    transpose x4 -> x0, local copies, waits for them, and re-layouts: 5.38 us -> none  [the longest x1 2.05 us: local(): step.reshape(32, 16, 16, 8).transpose(2, 1, 0, 3).reshape(16, 16, 256)]
    unnamed x12 -> x4, local copies, waits for them, and re-layouts: 6.54 us -> 2.37 us
    add x1 -> x0, other arithmetic: 3.14 us -> none  [local(): kernel + step.reshape(32, 16, 16, 8).transpose(2, 1, 0, 3).reshape(16, 16...]
    pallas_call x1 -> x0, local copies, waits for them, and re-layouts: 2.26 us -> none  [local(): pl.pallas_call(body, out_shape=(jax.ShapeDtypeStruct((32, 16, 128), F32),...]
    pallas_call x1, Pallas kernels: 96.1 us -> 93.9 us  [local(): pl.pallas_call(body, out_shape=(jax.ShapeDtypeStruct((16, 16, 256), F32),...]
where the time goes in v1:
time: 97 us; the launch traced here: 96.9 us
  Pallas kernels  93.9 us (97%)
  local copies, waits for them, and re-layouts  2.37 us (2%)
    pallas_call x1, Pallas kernels, local(): pl.pallas_call(body, out_shape=(jax.ShapeDtypeStruct((16, 16, 256), F32),...  93.9 us
    unnamed x4, local copies, waits for them, and re-layouts  2.37 us

profile of v1, /device:TPU:1, one launch (start us, length us, event | category | flops | bytes accessed | tf_op | source)
XLA Modules:
  0.0 96.9 jit_solution(13614960728793412866)
XLA Ops:
  0.6 93.9 %shard_map.50 = (f32[16,16,256]{2,1,0:T(8,128)}, bf16[32,2048]{1,0:T(8,128)(2,1)}) custom-call(bf16[16,2048]{1,0:T(8,128)(2,1)} %bitcast.3, bf16[2048,256]{1,0:T(8,128)(2,1)} %resp_hbm.1, f32[16,16,256]{2,1,0:T(8,128)} %ker_ref.1), custom_call_target="tpu_custom_call" | custom-call | tf_op jit(solution)/shard_map/pallas_call | solution.py:524
  94.5 0.0 copy-start
  94.5 1.7 %copy.7 = f32[16,16,256]{2,1,0:T(8,128)} copy(f32[16,16,256]{2,1,0:T(8,128)} %get-tuple-element.8) | data formatting | bytes 524288
  96.2 0.0 copy-done
  96.2 0.7 copy.8
Async XLA Ops:
  94.5 1.7 %copy-start = (bf16[32,2048]{1,0:T(8,128)(2,1)S(1)}, bf16[32,2048]{1,0:T(8,128)(2,1)}, u32[]{:S(2)}) copy-start(bf16[32,2048]{1,0:T(8,128)(2,1)} %get-tuple-element.5) | copy-start | bytes 393220

commit v2 on v1

--- a/solution.py
+++ b/solution.py
@@ -50,10 +50,10 @@
 def body(
     sig_ref, resp_hbm, ker_ref,
     kernel_ref, resid_ref,
-    gathered, rows, ker_tiles, resp_raw, resp_wide, resp_out, resid_wide, base,
-    sb, xe, weights, response, r_even, r_odd,
-    grad_out, grad_in, grad_own, grad_all, tiles, energy_a, energy_b, energy_own, acc, resid_all,
-    resid_in,
+    gathered, rows, halo, ker_tiles, resp_raw, resp_wide, resp_out, resid_wide, base,
+    sb, xe, taps, response, r_even, r_odd,
+    grad_out, grad_in, grad_own, tiles, factor_rows, energy_a, energy_b, energy_own, acc, resid_all,
+    resid_in, edge_t,
     hbm_sem, ker_send, ker_recv, resp_send, resp_recv, tail_send, tail_recv,
     za_send, za_recv, zh_send, zh_recv, xb_send, xb_recv, xa_send, xa_recv,
     zb_send, zb_recv, ca_send, ca_recv, cb_send, cb_recv,
@@ -106,7 +106,17 @@
     fetch = pltpu.make_async_copy(resp_hbm.at[:, columns], resp_raw, hbm_sem)
     fetch.start()
     row_z = pl.ds(pl.multiple_of(z * 16, 16), 16)
-    gathered[x_hi, core, x_lo, row_z, 256:2304] = sig_ref[...]
+    lane16 = lax.broadcasted_iota(jnp.int32, (16, 128), 1)
+    parts = [sig_ref[:, k * 128:(k + 1) * 128].astype(F32) for k in range(16)]
+    for bit in (1, 2, 4):
+        high = (lane16 & bit) != 0
+        for i in range(16):
+            if not i & (2 * bit):
+                one, two = parts[i], parts[i | (2 * bit)]
+                parts[i] = jnp.where(high, pltpu.roll(two, bit, axis=1), one)
+                parts[i | (2 * bit)] = jnp.where(high, two, pltpu.roll(one, 128 - bit, axis=1))
+    for k in range(16):
+        gathered[x_hi, core, x_lo, row_z, 256 + k * 128:384 + k * 128] = parts[k].astype(BF16)
     part_h, part_a, part_b = pl.ds(0, 256), pl.ds(256, 1024), pl.ds(1280, 1024)
     part_ha = pl.ds(0, 1280)
 
@@ -139,13 +149,13 @@
     def send_taps(r, carry):
         d = (rank + r) % 32
         remote(
-            ker_tiles.at[d], weights.at[y, pl.ds(row_k, 16), pl.ds(lane_k, 128)],
+            ker_tiles.at[d], taps.at[0, y, pl.ds(row_k, 16), pl.ds(lane_k, 128)],
             ker_send, ker_recv, in_plane(d),
         ).start()
         return carry
 
     lax.fori_loop(1, 32, send_taps, 0)
-    weights[y, pl.ds(row_k, 16), pl.ds(lane_k, 128)] = ker_tiles[rank]
+    taps[0, y, pl.ds(row_k, 16), pl.ds(lane_k, 128)] = ker_tiles[rank]
 
     tail_copy.wait()
     zh_copies = []
@@ -183,7 +193,7 @@
     w_copies = []
     for r in (2, 1, 3):
         w_copies.append(remote(
-            weights.at[y], weights.at[y], w_send.at[r - 1], w_recv.at[r - 1], along_y(r)
+            taps.at[0, y], taps.at[0, y], w_send.at[r - 1], w_recv.at[r - 1], along_y(r)
         ))
         w_copies[-1].start()
 
@@ -244,15 +254,15 @@
 
     def upright(hi, of_core):
         def one(k, carry):
-            lanes = pl.ds(pl.multiple_of(256 + k * 128, 128), 128)
-            block = jnp.concatenate(
-                [gathered[hi, of_core, 0, :, lanes], gathered[hi, of_core, 1, :, lanes]], axis=0
-            )
-            at = pl.multiple_of(256 + (hi * 2 + of_core) * 2048 + k * 128, 128)
-            rows[pl.ds(at, 128), :] = block.astype(F32).T
+            for m in range(8):
+                lanes = pl.ds(pl.multiple_of(256 + (k * 8 + m) * 128, 128), 128)
+                block = jnp.concatenate(
+                    [gathered[hi, of_core, 0, :, lanes], gathered[hi, of_core, 1, :, lanes]], axis=0
+                )
+                rows[hi * 2 + of_core, k * 8 + m] = block.T.astype(F32)
             return carry
 
-        lax.fori_loop(0, 16, one, 0)
+        lax.fori_loop(0, 2, one, 0)
 
     for hi in range(2):
         upright(hi, core)
@@ -265,18 +275,21 @@
         block = jnp.concatenate(
             [gathered[0, 0, lo, :, k * 128:(k + 1) * 128] for lo in range(2)], axis=0
         )
-        rows[k * 128:(k + 1) * 128, :] = jnp.where(at_start, 0.0, block.astype(F32).T)
+        halo[k * 128:(k + 1) * 128, :] = jnp.where(at_start, 0.0, block.astype(F32).T)
     for q in range(8):
-        xe[:, q * 128:(q + 1) * 128] = rows[(7 - q) * 32:(8 - q) * 32, :].astype(BF16)
+        xe[:, q * 128:(q + 1) * 128] = halo[(7 - q) * 32:(8 - q) * 32, :].astype(BF16)
+    first = lax.broadcasted_iota(jnp.int32, (32, 128), 0) == 0
 
     def order(p, carry):
         for b in range(8):
-            sb[p, b * 32:(b + 1) * 32, :] = rows[
-                pl.ds(b * 32 + p, 32, stride=256), :
-            ].astype(BF16)
-            sb[p, 256 + b * 32:256 + (b + 1) * 32, :] = rows[
-                pl.ds(256 + b * 32 + p, 32, stride=256), :
-            ].astype(BF16)
+            at = pl.multiple_of((b % 4) * 32 + (p // 8) * 8, 8)
+            block = jnp.concatenate(
+                [rows[g, (p % 8) * 2 + b // 4, pl.ds(at, 8), :] for g in range(4)], axis=0
+            )
+            edge = jnp.broadcast_to(halo[pl.ds(b * 32 + p, 1), :], (32, 128))
+            before = jnp.where(first, edge, pltpu.roll(block, 1, axis=0))
+            sb[p, b * 32:(b + 1) * 32, :] = before.astype(BF16)
+            sb[p, 256 + b * 32:256 + (b + 1) * 32, :] = block.astype(BF16)
         return carry
 
     lax.fori_loop(0, 32, order, 0)
@@ -289,9 +302,9 @@
     ext_lane = lax.broadcasted_iota(jnp.int32, (32, 256), 1)
     ext_row = lax.broadcasted_iota(jnp.int32, (32, 256), 0)
 
-    def forward(taps):
+    def forward(turn):
         def tap_matrix():
-            return jnp.concatenate([taps[j] for j in range(4)], axis=0)
+            return jnp.concatenate([taps[turn, j] for j in range(4)], axis=0)
 
         acc[...] = jnp.zeros_like(acc)
 
@@ -388,93 +401,125 @@
             rows_d = pl.multiple_of(((d % 4) // 2) * 128 + (to % 2) * 64 + (to // 2) * 16, 16)
             lanes = pl.ds(pl.multiple_of((d % 2) * 128, 128), 128)
             remote(
-                grad_all.at[turn, y, pl.ds(rows_d, 16), lanes], tiles.at[turn, rank],
+                taps.at[turn + 1, y, pl.ds(rows_d, 16), lanes], tiles.at[turn, rank],
                 t_send.at[turn], t_recv.at[turn], in_plane(d),
             ).start()
             return carry
 
         lax.fori_loop(1, 32, send, 0)
-        tiles[turn, rank] = grad_all[turn, y, pl.ds(row_k, 16), pl.ds(lane_k, 128)]
+        tiles[turn, rank] = taps[turn + 1, y, pl.ds(row_k, 16), pl.ds(lane_k, 128)]
+
+    def energy_copy(turn, r):
+        return remote(
+            energy_own.at[turn, 1], energy_b.at[turn, r - 1],
+            eb_send.at[turn, r - 1], eb_recv.at[turn, r - 1], along_y(r),
+        )
 
     def pass_energy(turn):
         mine = energy_a.at[turn]
         pltpu.make_async_copy(mine, mine, ea_recv.at[turn]).wait()
         energy_own[turn, 1] = energy_own[turn, 0] + jnp.sum(energy_a[turn], axis=0)
-        copies = []
         for r in (1, 2, 3):
-            copies.append(remote(
-                energy_own.at[turn, 1], energy_b.at[turn, r - 1],
-                eb_send.at[turn, r - 1], eb_recv.at[turn, r - 1], along_y(r),
-            ))
-            copies[-1].start()
-        return copies
-
-    def finish_energy(turn, copies):
-        for copy in copies:
-            copy.wait()
+            energy_copy(turn, r).start()
+
+    def finish_energy(turn):
+        for r in (1, 2, 3):
+            energy_copy(turn, r).wait()
         total = energy_own[turn, 1] + jnp.sum(energy_b[turn], axis=0)
-        factor = STEP_SIZE * lax.rsqrt(total / COUNT + EPSILON)
-        return factor[0:1, :]
-
-    factors = []
-    resid_copies = []
-    energy_copies = None
-    for turn in range(2):
-        if turn == 0:
-            predicted = forward(weights)
-            base[...] = predicted
-        else:
-            change = forward(grad_all.at[0])
-            factors.append(finish_energy(0, energy_copies))
-            wide = jnp.concatenate([factors[0], factors[0]], axis=1)
-            predicted = base[...] + wide * change
+        factor_rows[turn + 1] = STEP_SIZE * lax.rsqrt(total / COUNT + EPSILON)
+
+    def resid_copy(r):
+        there = pl.ds(pl.multiple_of(((s + r) % 4) * 8, 8), 8)
+        return remote(
+            resid_all.at[:, there, :], resid_in.at[s],
+            o_send.at[r - 1], o_recv.at[r - 1], in_group(r),
+        )
+
+    def shard_copy(turn, r):
+        return remote(
+            grad_out.at[r - 1], grad_in.at[r - 1],
+            rs_send.at[turn, r - 1], rs_recv.at[turn, r - 1], along_y(r),
+        )
+
+    def gather_copy(r):
+        return remote(
+            taps.at[1, y], taps.at[1, y], ag_send.at[r - 1], ag_recv.at[r - 1], along_y(r)
+        )
+
+    base[...] = jnp.zeros_like(base)
+    factor_rows[0] = jnp.ones((8, 128), F32)
+
+    def iterate(turn, carry):
+        change = forward(turn)
+
+        @pl.when(turn == 1)
+        def _():
+            finish_energy(0)
+
+        factor = factor_rows[turn, 0:1, :]
+        predicted = base[...] + jnp.concatenate([factor, factor], axis=1) * change
+        base[...] = predicted
         resid = (response[...].reshape(256, 256) - predicted).astype(BF16).astype(F32)
-        if turn == 1:
+
+        @pl.when(turn == 1)
+        def _():
             resid_all[...] = resid.reshape(8, 32, 256)
             for r in (1, 2, 3):
-                there = pl.ds(pl.multiple_of(((s + r) % 4) * 8, 8), 8)
-                resid_copies.append(remote(
-                    resid_all.at[:, there, :], resid_in.at[s],
-                    o_send.at[r - 1], o_recv.at[r - 1], in_group(r),
-                ))
-                resid_copies[-1].start()
+                resid_copy(r).start()
             resid_in[s] = resid_all[:, rows_s, :]
+
         expand(resid)
         flipped = edge_windows(resid)
-        edges = jnp.concatenate(
+        edge_t[...] = jnp.concatenate(
             [flipped[31 - j:32 - j, :] for j in range(32)], axis=0
         ).T.astype(BF16)
-        rs_copies = []
-        for r in (2, 1, 3):
-            grad_out[r - 1] = gradient_of((y + r) % 4, edges).astype(BF16)
-            rs_copies.append(remote(
-                grad_out.at[r - 1], grad_in.at[r - 1],
-                rs_send.at[turn, r - 1], rs_recv.at[turn, r - 1], along_y(r),
-            ))
-            rs_copies[-1].start()
-        own = gradient_of(y, edges)
-        for copy in rs_copies:
-            copy.wait()
+
+        def chunk(j, carry):
+            up = (6 - j) % 4
+            late = j // 2
+            r = up * (1 - late) + (3 - up) * late
+            part = gradient_of((y + r) % 4, edge_t[...])
+
+            @pl.when(j < 3)
+            def _():
+                grad_out[r - 1] = part.astype(BF16)
+                shard_copy(turn, r).start()
+
+            @pl.when(j == 3)
+            def _():
+                grad_own[...] = part
+
+            return carry
+
+        lax.fori_loop(0, 4, chunk, 0)
+        for r in (1, 3, 2):
+            shard_copy(turn, r).wait()
+        own = grad_own[...]
         for r in range(3):
             own = own + grad_in[r].astype(F32)
         grad_own[...] = own
-        grad_all[turn, y] = own.astype(BF16)
-        ag_copies = []
-        if turn == 0:
+        taps[turn + 1, y] = own.astype(BF16)
+
+        @pl.when(turn == 0)
+        def _():
             for r in (2, 1, 3):
-                ag_copies.append(remote(
-                    grad_all.at[turn, y], grad_all.at[turn, y],
-                    ag_send.at[r - 1], ag_recv.at[r - 1], along_y(r),
-                ))
-                ag_copies[-1].start()
+                gather_copy(r).start()
+
         send_energy(turn)
         send_tiles(turn)
-        energy_copies = pass_energy(turn)
-        for copy in ag_copies:
-            copy.wait()
-
-    for copy in resid_copies:
-        copy.wait()
+        pass_energy(turn)
+
+        @pl.when(turn == 0)
+        def _():
+            for r in (1, 3, 2):
+                gather_copy(r).wait()
+
+        return carry
+
+    lax.fori_loop(0, 2, iterate, 0)
+
+    for r in (1, 2, 3):
+        resid_copy(r).wait()
 
     def unpack_residual(b, carry):
         for half in range(2):
@@ -492,7 +537,8 @@
         flat = resid_wide[k * 128:(k + 1) * 128, :].T
         resid_ref[:, k * 128:(k + 1) * 128] = flat[0:32, :].astype(BF16)
 
-    factors.append(finish_energy(1, energy_copies))
+    finish_energy(1)
+    factors = [factor_rows[1, 0:1, :], factor_rows[2, 0:1, :]]
     for turn in range(2):
         half = tiles.at[turn, pl.ds(0, 31)]
         pltpu.make_async_copy(half, half, t_recv.at[turn]).wait()
@@ -531,7 +577,8 @@
         out_specs=(vmem, vmem),
         scratch_shapes=[
             pltpu.VMEM((2, 2, 2, 64, 2304), BF16),
-            pltpu.VMEM((8448, 128), F32),
+            pltpu.VMEM((4, 16, 128, 128), F32),
+            pltpu.VMEM((256, 128), F32),
             pltpu.VMEM((32, 16, 128), BF16),
             pltpu.VMEM((2048, 128), BF16),
             pltpu.VMEM((2048, 128), F32),
@@ -540,21 +587,22 @@
             pltpu.VMEM((256, 256), F32),
             pltpu.VMEM((32, 512, 128), BF16),
             pltpu.VMEM((32, 1024), BF16),
-            pltpu.VMEM((4, 256, 256), BF16),
+            pltpu.VMEM((3, 4, 256, 256), BF16),
             pltpu.VMEM((8, 32, 256), F32),
             pltpu.VMEM((512, 256), BF16),
             pltpu.VMEM((512, 256), BF16),
             pltpu.VMEM((3, 256, 256), BF16),
             pltpu.VMEM((3, 256, 256), BF16),
             pltpu.VMEM((256, 256), F32),
-            pltpu.VMEM((2, 4, 256, 256), BF16),
             pltpu.VMEM((2, 32, 16, 128), BF16),
+            pltpu.VMEM((3, 8, 128), F32),
             pltpu.VMEM((2, 31, 8, 128), F32),
             pltpu.VMEM((2, 3, 8, 128), F32),
             pltpu.VMEM((2, 2, 8, 128), F32),
             pltpu.VMEM((512, 256), F32),
             pltpu.VMEM((8, 32, 256), F32),
             pltpu.VMEM((4, 8, 8, 256), F32),
+            pltpu.VMEM((256, 32), BF16),
             dma, dma, dma, dma((3,)), dma((3,)), dma, dma,
             dma((3,)), dma((3,)), dma((3,)), dma((3,)), dma((3,)), dma((3,)), dma((3,)), dma((3,)),
             dma((4, 3)), dma((4, 3)), dma((4,)), dma((4,)), dma((4,)), dma((4,)),

time: 97 us -> 82.5 us (0.85)
  Pallas kernels: 93.9 us -> 79.4 us
    pallas_call x1, Pallas kernels: 93.9 us -> 79.4 us  [local(): pl.pallas_call(body, out_shape=(jax.ShapeDtypeStruct((16, 16, 256), F32),...]
where the time goes in v2:
time: 82.5 us; the launch traced here: 82.4 us
  Pallas kernels  79.4 us (96%)
  local copies, waits for them, and re-layouts  2.37 us (3%)
    pallas_call x1, Pallas kernels, local(): pl.pallas_call(body, out_shape=(jax.ShapeDtypeStruct((16, 16, 256), F32),...  79.4 us
    unnamed x4, local copies, waits for them, and re-layouts  2.37 us

profile of v2, /device:TPU:1, one launch (start us, length us, event | category | flops | bytes accessed | tf_op | source)
XLA Modules:
  0.0 82.4 jit_solution(10081535668167100996)
XLA Ops:
  0.6 79.4 %shard_map.50 = (f32[16,16,256]{2,1,0:T(8,128)}, bf16[32,2048]{1,0:T(8,128)(2,1)}) custom-call(bf16[16,2048]{1,0:T(8,128)(2,1)} %bitcast.3, bf16[2048,256]{1,0:T(8,128)(2,1)} %resp_hbm.1, f32[16,16,256]{2,1,0:T(8,128)} %ker_ref.1), custom_call_target="tpu_custom_call" | custom-call | tf_op jit(solution)/shard_map/pallas_call | solution.py:570
  80.0 0.0 copy-start
  80.0 1.7 %copy.7 = f32[16,16,256]{2,1,0:T(8,128)} copy(f32[16,16,256]{2,1,0:T(8,128)} %get-tuple-element.8) | data formatting | bytes 524288
  81.7 0.0 copy-done
  81.7 0.7 copy.8
Async XLA Ops:
  80.0 1.7 %copy-start = (bf16[32,2048]{1,0:T(8,128)(2,1)S(1)}, bf16[32,2048]{1,0:T(8,128)(2,1)}, u32[]{:S(2)}) copy-start(bf16[32,2048]{1,0:T(8,128)(2,1)} %get-tuple-element.5) | copy-start | bytes 393220

commit v3 on v2

--- a/solution.py
+++ b/solution.py
@@ -17,6 +17,7 @@
 CO = 256
 SCALE = 1.0 / math.sqrt(TAPS * CI)
 COUNT = TAPS * CI * CO
+WIDE = 16
 
 
 def remote(src, dst, send, recv, device):
@@ -56,7 +57,7 @@
     resid_in, edge_t,
     hbm_sem, ker_send, ker_recv, resp_send, resp_recv, tail_send, tail_recv,
     za_send, za_recv, zh_send, zh_recv, xb_send, xb_recv, xa_send, xa_recv,
-    zb_send, zb_recv, ca_send, ca_recv, cb_send, cb_recv,
+    xh_send, xh_recv, ch_send, ch_recv, zb_send, zb_recv, ca_send, ca_recv, cb_send, cb_recv,
     w_send, w_recv, rs_send, rs_recv, ag_send, ag_recv,
     ea_send, ea_recv, eb_send, eb_recv, t_send, t_recv, o_send, o_recv,
 ):
@@ -98,9 +99,6 @@
     lax.fori_loop(1, 32, greet, 0)
     for r in (1, 2, 3):
         pl.semaphore_signal(barrier, inc=1, device_id=along_y(r), device_id_type=MESH)
-    pl.semaphore_signal(
-        barrier, inc=1, device_id=((tm + 15) % 16, inch), device_id_type=MESH
-    )
 
     columns = pl.ds(pl.multiple_of((inch // 4) * 128, 128), 128)
     fetch = pltpu.make_async_copy(resp_hbm.at[:, columns], resp_raw, hbm_sem)
@@ -118,15 +116,12 @@
     for k in range(16):
         gathered[x_hi, core, x_lo, row_z, 256 + k * 128:384 + k * 128] = parts[k].astype(BF16)
     part_h, part_a, part_b = pl.ds(0, 256), pl.ds(256, 1024), pl.ds(1280, 1024)
-    part_ha = pl.ds(0, 1280)
-
-    pl.semaphore_wait(barrier, 35)
-
-    nxt = (tm + 1) % 16
+
+    pl.semaphore_wait(barrier, 34)
+
+    own_halo = gathered.at[x_hi, core, x_lo, row_z, part_h]
     tail_copy = remote(
-        sig_ref.at[:, pl.ds(1792, 256)],
-        gathered.at[(nxt % 4) // 2, nxt % 2, x_lo, row_z, part_h],
-        tail_send, tail_recv, (nxt, inch),
+        sig_ref.at[:, pl.ds(1792, 256)], own_halo, tail_send, tail_recv, along_y(1)
     )
     tail_copy.start()
     za_copies = []
@@ -177,16 +172,23 @@
 
     place = {2: 0, 1: 1, 3: 2}
     pass_b(0)
-    for copy in za_copies + zh_copies:
+    for copy in za_copies:
         copy.wait_recv()
     xa_copies = []
     for r in (2, 1, 3):
-        view = gathered.at[x_hi, core, x_lo, :, part_ha]
+        view = gathered.at[x_hi, core, x_lo, :, part_a]
         xa_copies.append(remote(view, view, xa_send.at[r - 1], xa_recv.at[r - 1], along_x(r)))
         xa_copies[-1].start()
     for r in (1, 3, 2):
         xb_copies[place[r]].wait_recv()
         pass_b(r)
+    for copy in zh_copies:
+        copy.wait_recv()
+    xh_copies = []
+    for r in (2, 1, 3):
+        view = gathered.at[x_hi, core, x_lo, :, part_h]
+        xh_copies.append(remote(view, view, xh_send.at[r - 1], xh_recv.at[r - 1], along_x(r)))
+        xh_copies[-1].start()
 
     all_tiles = ker_tiles.at[pl.ds(0, 31)]
     pltpu.make_async_copy(all_tiles, all_tiles, ker_recv).wait()
@@ -243,7 +245,7 @@
         there = (x + 4 - r) % 4
         if r:
             xa_copies[place[r]].wait_recv()
-        view = gathered.at[there // 2, core, there % 2, :, part_ha]
+        view = gathered.at[there // 2, core, there % 2, :, part_a]
         ca_copies.append(remote(view, view, ca_send.at[r], ca_recv.at[r], other))
         ca_copies[-1].start()
         for k in (1, 2, 3):
@@ -251,6 +253,13 @@
         view = gathered.at[there // 2, core, there % 2, :, part_b]
         cb_copies.append(remote(view, view, cb_send.at[r], cb_recv.at[r], other))
         cb_copies[-1].start()
+    for copy in xh_copies:
+        copy.wait_recv()
+    ch_copies = []
+    for lo in range(2):
+        view = gathered.at[1, core, lo, :, part_h]
+        ch_copies.append(remote(view, view, ch_send.at[lo], ch_recv.at[lo], other))
+        ch_copies[-1].start()
 
     def upright(hi, of_core):
         def one(k, carry):
@@ -266,14 +275,14 @@
 
     for hi in range(2):
         upright(hi, core)
-    for copy in ca_copies + cb_copies:
+    for copy in ca_copies + cb_copies + ch_copies:
         copy.wait_recv()
     for hi in range(2):
         upright(hi, 1 - core)
     at_start = y == 0
     for k in range(2):
         block = jnp.concatenate(
-            [gathered[0, 0, lo, :, k * 128:(k + 1) * 128] for lo in range(2)], axis=0
+            [gathered[1, 1, lo, :, k * 128:(k + 1) * 128] for lo in range(2)], axis=0
         )
         halo[k * 128:(k + 1) * 128, :] = jnp.where(at_start, 0.0, block.astype(F32).T)
     for q in range(8):
@@ -312,18 +321,18 @@
             lhs = jnp.concatenate(
                 [
                     jnp.concatenate(
-                        [sb[g * 4 + j, (8 - q) * 32:(8 - q) * 32 + 256, :] for q in range(8)],
+                        [sb[g * WIDE + j, (8 - q) * 32:(8 - q) * 32 + 256, :] for q in range(8)],
                         axis=1,
                     )
-                    for j in range(4)
+                    for j in range(WIDE)
                 ],
                 axis=0,
             )
             product = jnp.dot(lhs, tap_matrix(), preferred_element_type=F32)
             here = acc[0:256, :]
             after = acc[256:512, :]
-            for j in range(4):
-                shift = (g * 4 + j) * 8
+            for j in range(WIDE):
+                shift = (g * WIDE + j) * 8
                 turned = pltpu.roll(product[j * 256:(j + 1) * 256], shift, axis=1)
                 keep = wide_lane >= shift
                 here = here + jnp.where(keep, turned, 0.0)
@@ -332,7 +341,7 @@
             acc[256:512, :] = after
             return carry
 
-        lax.fori_loop(0, 8, group, 0)
+        lax.fori_loop(0, 32 // WIDE, group, 0)
         edge = jnp.dot(xe[...], tap_matrix(), preferred_element_type=F32)
         edge = pltpu.roll(edge, 0, axis=1, stride=8, stride_axis=0)
         edge = jnp.sum(jnp.where(ext_lane < ext_row * 8, edge, 0.0), axis=0, keepdims=True)
@@ -359,10 +368,10 @@
         line = pltpu.roll(line, 8, axis=1, stride=8, stride_axis=0)
         return jnp.where(ext_lane + (31 - ext_row) * 8 >= 256, line, 0.0)
 
-    def gradient_of(there, edges):
+    def gradient_of(one, two, edges):
         total = jnp.zeros((256, 256), F32)
-        top = pl.multiple_of((8 - 2 * there) * 32, 32)
-        low = pl.multiple_of((7 - 2 * there) * 32, 32)
+        first_at = pl.multiple_of((8 - one) * 32, 32)
+        second_at = pl.multiple_of((8 - two) * 32, 32)
         for g in range(8):
             left = []
             right = []
@@ -371,14 +380,20 @@
                 at = 8 * (p - p % 2)
                 left.append(windows[at:at + 256, :])
                 right.append(jnp.concatenate(
-                    [sb[p, pl.ds(top, 256), :], sb[p, pl.ds(low, 256), :]], axis=1
+                    [sb[p, pl.ds(first_at, 256), :], sb[p, pl.ds(second_at, 256), :]], axis=1
                 ))
             total = total + jnp.dot(
                 jnp.concatenate(left, axis=1), jnp.concatenate(right, axis=0),
                 preferred_element_type=F32,
             )
-        lanes = pl.ds(pl.multiple_of(there * 256, 256), 256)
-        total = total + jnp.dot(edges, xe[:, lanes], preferred_element_type=F32)
+        edge_rows = jnp.concatenate(
+            [
+                xe[:, pl.ds(pl.multiple_of(one * 128, 128), 128)],
+                xe[:, pl.ds(pl.multiple_of(two * 128, 128), 128)],
+            ],
+            axis=1,
+        )
+        total = total + jnp.dot(edges, edge_rows, preferred_element_type=F32)
         return total.T * SCALE
 
     def send_energy(turn):
@@ -435,16 +450,16 @@
             o_send.at[r - 1], o_recv.at[r - 1], in_group(r),
         )
 
-    def shard_copy(turn, r):
+    def shard_copy(turn, half, r):
+        at = pl.ds(pl.multiple_of(half * 128, 128), 128)
         return remote(
-            grad_out.at[r - 1], grad_in.at[r - 1],
-            rs_send.at[turn, r - 1], rs_recv.at[turn, r - 1], along_y(r),
-        )
-
-    def gather_copy(r):
-        return remote(
-            taps.at[1, y], taps.at[1, y], ag_send.at[r - 1], ag_recv.at[r - 1], along_y(r)
-        )
+            grad_out.at[r - 1, at], grad_in.at[r - 1, at],
+            rs_send.at[turn, half, r - 1], rs_recv.at[turn, half, r - 1], along_y(r),
+        )
+
+    def gather_copy(half, r):
+        view = taps.at[1, y, pl.ds(half * 128, 128)]
+        return remote(view, view, ag_send.at[half, r - 1], ag_recv.at[half, r - 1], along_y(r))
 
     base[...] = jnp.zeros_like(base)
     factor_rows[0] = jnp.ones((8, 128), F32)
@@ -475,35 +490,43 @@
         ).T.astype(BF16)
 
         def chunk(j, carry):
-            up = (6 - j) % 4
-            late = j // 2
-            r = up * (1 - late) + (3 - up) * late
-            part = gradient_of((y + r) % 4, edge_t[...])
-
-            @pl.when(j < 3)
+            half = j // 2
+            late = j % 2
+            ahead = 2 + late
+            beside = 1 - late
+            part = gradient_of(
+                (y + ahead) % 4 * 2 + half, (y + beside) % 4 * 2 + half, edge_t[...]
+            )
+            at = pl.ds(pl.multiple_of(half * 128, 128), 128)
+            grad_out[ahead - 1, at] = part[0:128].astype(BF16)
+            shard_copy(turn, half, ahead).start()
+
+            @pl.when(late == 0)
             def _():
-                grad_out[r - 1] = part.astype(BF16)
-                shard_copy(turn, r).start()
-
-            @pl.when(j == 3)
+                grad_out[0, at] = part[128:256].astype(BF16)
+                shard_copy(turn, half, 1).start()
+
+            @pl.when(late == 1)
             def _():
-                grad_own[...] = part
+                grad_own[at, :] = part[128:256]
 
             return carry
 
         lax.fori_loop(0, 4, chunk, 0)
-        for r in (1, 3, 2):
-            shard_copy(turn, r).wait()
-        own = grad_own[...]
-        for r in range(3):
-            own = own + grad_in[r].astype(F32)
-        grad_own[...] = own
-        taps[turn + 1, y] = own.astype(BF16)
-
-        @pl.when(turn == 0)
-        def _():
-            for r in (2, 1, 3):
-                gather_copy(r).start()
+        for half in range(2):
+            at = slice(half * 128, (half + 1) * 128)
+            for r in (1, 2, 3):
+                shard_copy(turn, half, r).wait()
+            own = grad_own[at, :]
+            for r in range(3):
+                own = own + grad_in[r, at].astype(F32)
+            grad_own[at, :] = own
+            taps[turn + 1, y, at] = own.astype(BF16)
+
+            @pl.when(turn == 0)
+            def _(half=half):
+                for r in (2, 1, 3):
+                    gather_copy(half, r).start()
 
         send_energy(turn)
         send_tiles(turn)
@@ -511,8 +534,9 @@
 
         @pl.when(turn == 0)
         def _():
-            for r in (1, 3, 2):
-                gather_copy(r).wait()
+            for half in range(2):
+                for r in (1, 3, 2):
+                    gather_copy(half, r).wait()
 
         return carry
 
@@ -553,7 +577,7 @@
             kernel_ref[u, :, lanes] = ker_ref[u, :, lanes] + step
 
     pltpu.make_async_copy(all_tiles, all_tiles, ker_send).wait()
-    for copy in za_copies + zh_copies + xb_copies + xa_copies + ca_copies + cb_copies:
+    for copy in za_copies + zh_copies + xb_copies + xa_copies + xh_copies + ca_copies + cb_copies + ch_copies:
         copy.wait_send()
     for copy in zb_copies.values():
         copy.wait_send()
@@ -605,8 +629,8 @@
             pltpu.VMEM((256, 32), BF16),
             dma, dma, dma, dma((3,)), dma((3,)), dma, dma,
             dma((3,)), dma((3,)), dma((3,)), dma((3,)), dma((3,)), dma((3,)), dma((3,)), dma((3,)),
-            dma((4, 3)), dma((4, 3)), dma((4,)), dma((4,)), dma((4,)), dma((4,)),
-            dma((3,)), dma((3,)), dma((2, 3)), dma((2, 3)), dma((3,)), dma((3,)),
+            dma((3,)), dma((3,)), dma((2,)), dma((2,)), dma((4, 3)), dma((4, 3)), dma((4,)), dma((4,)), dma((4,)), dma((4,)),
+            dma((3,)), dma((3,)), dma((2, 2, 3)), dma((2, 2, 3)), dma((2, 3)), dma((2, 3)),
             dma((2,)), dma((2,)), dma((2, 3)), dma((2, 3)), dma((2,)), dma((2,)), dma((3,)), dma((3,)),
         ],
         compiler_params=pltpu.CompilerParams(

time: 82.5 us -> 77 us (0.933)
  Pallas kernels: 79.4 us -> 73.7 us
    pallas_call x1, Pallas kernels: 79.4 us -> 73.7 us  [local(): pl.pallas_call(body, out_shape=(jax.ShapeDtypeStruct((16, 16, 256), F32),...]
where the time goes in v3:
time: 77 us; the launch traced here: 76.8 us
  Pallas kernels  73.7 us (96%)
  local copies, waits for them, and re-layouts  2.37 us (3%)
    pallas_call x1, Pallas kernels, local(): pl.pallas_call(body, out_shape=(jax.ShapeDtypeStruct((16, 16, 256), F32),...  73.7 us
    unnamed x4, local copies, waits for them, and re-layouts  2.37 us

profile of v3, /device:TPU:1, one launch (start us, length us, event | category | flops | bytes accessed | tf_op | source)
XLA Modules:
  0.0 76.8 jit_solution(6813745247808375202)
XLA Ops:
  0.6 73.7 %shard_map.50 = (f32[16,16,256]{2,1,0:T(8,128)}, bf16[32,2048]{1,0:T(8,128)(2,1)}) custom-call(bf16[16,2048]{1,0:T(8,128)(2,1)} %bitcast.3, bf16[2048,256]{1,0:T(8,128)(2,1)} %resp_hbm.1, f32[16,16,256]{2,1,0:T(8,128)} %ker_ref.1), custom_call_target="tpu_custom_call" | custom-call | tf_op jit(solution)/shard_map/pallas_call | solution.py:594
  74.4 0.0 copy-start
  74.4 1.7 %copy.7 = f32[16,16,256]{2,1,0:T(8,128)} copy(f32[16,16,256]{2,1,0:T(8,128)} %get-tuple-element.8) | data formatting | bytes 524288
  76.1 0.0 copy-done
  76.1 0.7 copy.8
Async XLA Ops:
  74.4 1.7 %copy-start = (bf16[32,2048]{1,0:T(8,128)(2,1)S(1)}, bf16[32,2048]{1,0:T(8,128)(2,1)}, u32[]{:S(2)}) copy-start(bf16[32,2048]{1,0:T(8,128)(2,1)} %get-tuple-element.5) | copy-start | bytes 393220

commit v4 on v3

--- a/solution.py
+++ b/solution.py
@@ -17,7 +17,6 @@
 CO = 256
 SCALE = 1.0 / math.sqrt(TAPS * CI)
 COUNT = TAPS * CI * CO
-WIDE = 16
 
 
 def remote(src, dst, send, recv, device):
@@ -49,12 +48,13 @@
 
 
 def body(
-    sig_ref, resp_hbm, ker_ref,
+    sig_hbm, resp_hbm, ker_hbm,
     kernel_ref, resid_ref,
     gathered, rows, halo, ker_tiles, resp_raw, resp_wide, resp_out, resid_wide, base,
     sb, xe, taps, response, r_even, r_odd,
-    grad_out, grad_in, grad_own, tiles, factor_rows, energy_a, energy_b, energy_own, acc, resid_all,
+    grad_out, grad_in, grad_own, tiles, factor_rows, energy_a, energy_b, energy_own, resid_all,
     resid_in, edge_t,
+    sig_ref, ker_ref, in_sem,
     hbm_sem, ker_send, ker_recv, resp_send, resp_recv, tail_send, tail_recv,
     za_send, za_recv, zh_send, zh_recv, xb_send, xb_recv, xa_send, xa_recv,
     xh_send, xh_recv, ch_send, ch_recv, zb_send, zb_recv, ca_send, ca_recv, cb_send, cb_recv,
@@ -100,10 +100,15 @@
     for r in (1, 2, 3):
         pl.semaphore_signal(barrier, inc=1, device_id=along_y(r), device_id_type=MESH)
 
+    take_sig = pltpu.make_async_copy(sig_hbm, sig_ref, in_sem.at[0])
+    take_sig.start()
+    take_ker = pltpu.make_async_copy(ker_hbm, ker_ref, in_sem.at[1])
+    take_ker.start()
     columns = pl.ds(pl.multiple_of((inch // 4) * 128, 128), 128)
     fetch = pltpu.make_async_copy(resp_hbm.at[:, columns], resp_raw, hbm_sem)
     fetch.start()
     row_z = pl.ds(pl.multiple_of(z * 16, 16), 16)
+    take_sig.wait()
     lane16 = lax.broadcasted_iota(jnp.int32, (16, 128), 1)
     parts = [sig_ref[:, k * 128:(k + 1) * 128].astype(F32) for k in range(16)]
     for bit in (1, 2, 4):
@@ -134,6 +139,7 @@
         xb_copies.append(remote(view, view, xb_send.at[r - 1], xb_recv.at[r - 1], along_x(r)))
         xb_copies[-1].start()
 
+    take_ker.wait()
     for half in range(2):
         swapped = swap_blocks([ker_ref[u, :, half * 128:(half + 1) * 128] for u in range(16)])
         for d in range(16):
@@ -315,42 +321,31 @@
         def tap_matrix():
             return jnp.concatenate([taps[turn, j] for j in range(4)], axis=0)
 
-        acc[...] = jnp.zeros_like(acc)
-
-        def group(g, carry):
-            lhs = jnp.concatenate(
-                [
-                    jnp.concatenate(
-                        [sb[g * WIDE + j, (8 - q) * 32:(8 - q) * 32 + 256, :] for q in range(8)],
-                        axis=1,
-                    )
-                    for j in range(WIDE)
-                ],
-                axis=0,
-            )
-            product = jnp.dot(lhs, tap_matrix(), preferred_element_type=F32)
-            here = acc[0:256, :]
-            after = acc[256:512, :]
-            for j in range(WIDE):
-                shift = (g * WIDE + j) * 8
-                turned = pltpu.roll(product[j * 256:(j + 1) * 256], shift, axis=1)
-                keep = wide_lane >= shift
-                here = here + jnp.where(keep, turned, 0.0)
-                after = after + jnp.where(keep, 0.0, turned)
-            acc[0:256, :] = here
-            acc[256:512, :] = after
-            return carry
-
-        lax.fori_loop(0, 32 // WIDE, group, 0)
+        lhs = jnp.concatenate(
+            [
+                jnp.concatenate(
+                    [sb[p, (8 - q) * 32:(8 - q) * 32 + 256, :] for q in range(8)], axis=1
+                )
+                for p in range(32)
+            ],
+            axis=0,
+        )
+        product = jnp.dot(lhs, tap_matrix(), preferred_element_type=F32)
+        here = product[0:256]
+        after = jnp.zeros((256, 256), F32)
+        for p in range(1, 32):
+            turned = pltpu.roll(product[p * 256:(p + 1) * 256], 8 * p, axis=1)
+            keep = wide_lane >= 8 * p
+            here = here + jnp.where(keep, turned, 0.0)
+            after = after + jnp.where(keep, 0.0, turned)
         edge = jnp.dot(xe[...], tap_matrix(), preferred_element_type=F32)
         edge = pltpu.roll(edge, 0, axis=1, stride=8, stride_axis=0)
         edge = jnp.sum(jnp.where(ext_lane < ext_row * 8, edge, 0.0), axis=0, keepdims=True)
-        after = acc[256:512, :]
         moved = jnp.where(
             wide_row >= 32, pltpu.roll(after, 32, axis=0), pltpu.roll(after, 33, axis=0)
         )
         moved = jnp.where(wide_row == 0, jnp.broadcast_to(edge, (256, 256)), moved)
-        return (acc[0:256, :] + moved) * SCALE
+        return (here + moved) * SCALE
 
     def expand(resid):
         later = jnp.where(
@@ -513,6 +508,11 @@
             return carry
 
         lax.fori_loop(0, 4, chunk, 0)
+
+        @pl.when(turn == 1)
+        def _():
+            send_tiles(0)
+
         for half in range(2):
             at = slice(half * 128, (half + 1) * 128)
             for r in (1, 2, 3):
@@ -529,7 +529,11 @@
                     gather_copy(half, r).start()
 
         send_energy(turn)
-        send_tiles(turn)
+
+        @pl.when(turn == 1)
+        def _():
+            send_tiles(1)
+
         pass_energy(turn)
 
         @pl.when(turn == 0)
@@ -574,7 +578,7 @@
         ]
         lanes = slice(half * 128, (half + 1) * 128)
         for u, step in enumerate(swap_blocks(steps)):
-            kernel_ref[u, :, lanes] = ker_ref[u, :, lanes] + step
+            kernel_ref[u, :, lanes] = step
 
     pltpu.make_async_copy(all_tiles, all_tiles, ker_send).wait()
     for copy in za_copies + zh_copies + xb_copies + xa_copies + xh_copies + ca_copies + cb_copies + ch_copies:
@@ -588,6 +592,11 @@
         pltpu.make_async_copy(half, half, t_send.at[turn]).wait()
 
 
+def finish(step_ref, ker_ref, resid_in_ref, kernel_ref, resid_ref):
+    kernel_ref[...] = ker_ref[...] + step_ref[...]
+    resid_ref[...] = resid_in_ref[...]
+
+
 def local(signal, response, kernel):
     dma = pltpu.SemaphoreType.DMA
     vmem = pl.BlockSpec(memory_space=pltpu.VMEM)
@@ -597,7 +606,7 @@
             jax.ShapeDtypeStruct((16, 16, 256), F32),
             jax.ShapeDtypeStruct((32, 2048), BF16),
         ),
-        in_specs=[vmem, pl.BlockSpec(memory_space=pl.ANY), vmem],
+        in_specs=[pl.BlockSpec(memory_space=pl.ANY)] * 3,
         out_specs=(vmem, vmem),
         scratch_shapes=[
             pltpu.VMEM((2, 2, 2, 64, 2304), BF16),
@@ -623,10 +632,12 @@
             pltpu.VMEM((2, 31, 8, 128), F32),
             pltpu.VMEM((2, 3, 8, 128), F32),
             pltpu.VMEM((2, 2, 8, 128), F32),
-            pltpu.VMEM((512, 256), F32),
             pltpu.VMEM((8, 32, 256), F32),
             pltpu.VMEM((4, 8, 8, 256), F32),
             pltpu.VMEM((256, 32), BF16),
+            pltpu.VMEM((16, 2048), BF16),
+            pltpu.VMEM((16, 16, 256), F32),
+            dma((2,)),
             dma, dma, dma, dma((3,)), dma((3,)), dma, dma,
             dma((3,)), dma((3,)), dma((3,)), dma((3,)), dma((3,)), dma((3,)), dma((3,)), dma((3,)),
             dma((3,)), dma((3,)), dma((2,)), dma((2,)), dma((4, 3)), dma((4, 3)), dma((4,)), dma((4,)), dma((4,)), dma((4,)),
@@ -637,6 +648,15 @@
             collective_id=0, has_side_effects=True, vmem_limit_bytes=60 * 2**20
         ),
     )(signal.T, response, kernel)
+    kernel_out, resid = pl.pallas_call(
+        finish,
+        out_shape=(
+            jax.ShapeDtypeStruct((16, 16, 256), F32),
+            jax.ShapeDtypeStruct((32, 2048), BF16),
+        ),
+        in_specs=[vmem] * 3,
+        out_specs=(vmem, vmem),
+    )(kernel_out, kernel, resid)
     return kernel_out, resid.T
 
 

time: 77 us -> 74.4 us (0.966)
  local copies, waits for them, and re-layouts: 2.37 us -> 0 us
    unnamed x4 -> x0, local copies, waits for them, and re-layouts: 2.37 us -> none
    pallas_call x1, Pallas kernels: 73.7 us -> 71.8 us  [local(): pl.pallas_call(body, out_shape=(jax.ShapeDtypeStruct((16, 16, 256), F32),...]
    pallas_call x0 -> x1, Pallas kernels: none -> 1.83 us  [local(): pl.pallas_call(finish, out_shape=(jax.ShapeDtypeStruct((16, 16, 256), F32...]
where the time goes in v4:
time: 74.4 us; the launch traced here: 74.3 us
  Pallas kernels  73.6 us (99%)
    pallas_call x1, Pallas kernels, local(): pl.pallas_call(body, out_shape=(jax.ShapeDtypeStruct((16, 16, 256), F32),...  71.8 us
    pallas_call x1, Pallas kernels, local(): pl.pallas_call(finish, out_shape=(jax.ShapeDtypeStruct((16, 16, 256), F32...  1.83 us

profile of v4, /device:TPU:1, one launch (start us, length us, event | category | flops | bytes accessed | tf_op | source)
XLA Modules:
  0.0 74.3 jit_solution(6843520379614160360)
XLA Ops:
  0.6 71.8 %shard_map.50 = (f32[16,16,256]{2,1,0:T(8,128)}, bf16[32,2048]{1,0:T(8,128)(2,1)}) custom-call(bf16[16,2048]{1,0:T(8,128)(2,1)} %bitcast.2, bf16[2048,256]{1,0:T(8,128)(2,1)} %resp_hbm.1, f32[16,16,256]{2,1,0:T(8,128)} %ker_ref.1), custom_call_target="tpu_custom_call" | custom-call | tf_op jit(solution)/shard_map/pallas_call | solution.py:603
  72.4 1.8 %shard_map.51 = (f32[16,16,256]{2,1,0:T(8,128)}, bf16[32,2048]{1,0:T(8,128)(2,1)}) custom-call(f32[16,16,256]{2,1,0:T(8,128)} %get-tuple-element.6.step_ref, f32[16,16,256]{2,1,0:T(8,128)} %ker_ref.1, bf16[32,2048]{1,0:T(8,128)(2,1)} %get-tuple-element.7.resid_in_ref), custom_call_target="tpu_custom_call" | custom-call | tf_op jit(solution)/shard_map/pallas_call | solution.py:651

commit v5 on v4

--- a/solution.py
+++ b/solution.py
@@ -56,8 +56,8 @@
     resid_in, edge_t,
     sig_ref, ker_ref, in_sem,
     hbm_sem, ker_send, ker_recv, resp_send, resp_recv, tail_send, tail_recv,
-    za_send, za_recv, zh_send, zh_recv, xb_send, xb_recv, xa_send, xa_recv,
-    xh_send, xh_recv, ch_send, ch_recv, zb_send, zb_recv, ca_send, ca_recv, cb_send, cb_recv,
+    za_send, za_recv, xb_send, xb_recv, xa_send, xa_recv,
+    halo_send, halo_recv, zb_send, zb_recv, ca_send, ca_recv, cb_send, cb_recv,
     w_send, w_recv, rs_send, rs_recv, ag_send, ag_recv,
     ea_send, ea_recv, eb_send, eb_recv, t_send, t_recv, o_send, o_recv,
 ):
@@ -81,6 +81,12 @@
     def along_z(r):
         return (tm, ((z + r) % 4) * 2 + x_lo)
 
+    def diagonal(r, k):
+        return (((y + r) % 4) * 4 + s, ((z + k) % 4) * 2 + x_lo)
+
+    def in_row(g):
+        return (y * 4 + (g // 4) * 2 + g % 2, z * 2 + (g // 2) % 2)
+
     def along_x(r):
         there = (x + r) % 4
         return (y * 4 + (there // 2) * 2 + core, z * 2 + there % 2)
@@ -99,6 +105,7 @@
     lax.fori_loop(1, 32, greet, 0)
     for r in (1, 2, 3):
         pl.semaphore_signal(barrier, inc=1, device_id=along_y(r), device_id_type=MESH)
+        pl.semaphore_signal(barrier, inc=1, device_id=diagonal(3, r), device_id_type=MESH)
 
     take_sig = pltpu.make_async_copy(sig_hbm, sig_ref, in_sem.at[0])
     take_sig.start()
@@ -122,13 +129,16 @@
         gathered[x_hi, core, x_lo, row_z, 256 + k * 128:384 + k * 128] = parts[k].astype(BF16)
     part_h, part_a, part_b = pl.ds(0, 256), pl.ds(256, 1024), pl.ds(1280, 1024)
 
-    pl.semaphore_wait(barrier, 34)
+    pl.semaphore_wait(barrier, 37)
 
     own_halo = gathered.at[x_hi, core, x_lo, row_z, part_h]
-    tail_copy = remote(
-        sig_ref.at[:, pl.ds(1792, 256)], own_halo, tail_send, tail_recv, along_y(1)
-    )
-    tail_copy.start()
+    tail_copies = []
+    for k in (2, 1, 3, 0):
+        tail_copies.append(remote(
+            sig_ref.at[:, pl.ds(1792, 256)], own_halo,
+            tail_send.at[k], tail_recv.at[k], diagonal(1, k),
+        ))
+        tail_copies[-1].start()
     za_copies = []
     xb_copies = []
     for r in (2, 1, 3):
@@ -158,13 +168,6 @@
     lax.fori_loop(1, 32, send_taps, 0)
     taps[0, y, pl.ds(row_k, 16), pl.ds(lane_k, 128)] = ker_tiles[rank]
 
-    tail_copy.wait()
-    zh_copies = []
-    for r in (2, 1, 3):
-        view = gathered.at[x_hi, core, x_lo, row_z, part_h]
-        zh_copies.append(remote(view, view, zh_send.at[r - 1], zh_recv.at[r - 1], along_z(r)))
-        zh_copies[-1].start()
-
     other = (y * 4 + x_hi * 2 + 1 - core, inch)
     zb_copies = {}
 
@@ -185,16 +188,26 @@
         view = gathered.at[x_hi, core, x_lo, :, part_a]
         xa_copies.append(remote(view, view, xa_send.at[r - 1], xa_recv.at[r - 1], along_x(r)))
         xa_copies[-1].start()
+    view = gathered.at[x_hi, core, x_lo, :, part_a]
+    ca_copies = [remote(view, view, ca_send.at[0], ca_recv.at[0], other)]
+    ca_copies[0].start()
     for r in (1, 3, 2):
         xb_copies[place[r]].wait_recv()
         pass_b(r)
-    for copy in zh_copies:
-        copy.wait_recv()
-    xh_copies = []
-    for r in (2, 1, 3):
-        view = gathered.at[x_hi, core, x_lo, :, part_h]
-        xh_copies.append(remote(view, view, xh_send.at[r - 1], xh_recv.at[r - 1], along_x(r)))
-        xh_copies[-1].start()
+
+    for copy in tail_copies:
+        copy.wait()
+
+    def halo_copy(lo, r):
+        view = gathered.at[1, 1, lo, :, part_h]
+        return remote(
+            view, view, halo_send.at[r - 1], halo_recv.at[lo], in_row((x * 2 + core + r) % 8)
+        )
+
+    @pl.when(s == 3)
+    def _():
+        for r in range(1, 8):
+            halo_copy(x_lo, r).start()
 
     all_tiles = ker_tiles.at[pl.ds(0, 31)]
     pltpu.make_async_copy(all_tiles, all_tiles, ker_recv).wait()
@@ -245,27 +258,20 @@
         resp_copies[-1].start()
     response[:, rows_s, :] = resp_out[s]
 
-    ca_copies = []
     cb_copies = []
     for r in (0, 1, 3, 2):
         there = (x + 4 - r) % 4
         if r:
             xa_copies[place[r]].wait_recv()
-        view = gathered.at[there // 2, core, there % 2, :, part_a]
-        ca_copies.append(remote(view, view, ca_send.at[r], ca_recv.at[r], other))
-        ca_copies[-1].start()
+        if r:
+            view = gathered.at[there // 2, core, there % 2, :, part_a]
+            ca_copies.append(remote(view, view, ca_send.at[r], ca_recv.at[r], other))
+            ca_copies[-1].start()
         for k in (1, 2, 3):
             zb_copies[r, k].wait_recv()
         view = gathered.at[there // 2, core, there % 2, :, part_b]
         cb_copies.append(remote(view, view, cb_send.at[r], cb_recv.at[r], other))
         cb_copies[-1].start()
-    for copy in xh_copies:
-        copy.wait_recv()
-    ch_copies = []
-    for lo in range(2):
-        view = gathered.at[1, core, lo, :, part_h]
-        ch_copies.append(remote(view, view, ch_send.at[lo], ch_recv.at[lo], other))
-        ch_copies[-1].start()
 
     def upright(hi, of_core):
         def one(k, carry):
@@ -281,10 +287,16 @@
 
     for hi in range(2):
         upright(hi, core)
-    for copy in ca_copies + cb_copies + ch_copies:
+    for copy in ca_copies + cb_copies:
         copy.wait_recv()
     for hi in range(2):
         upright(hi, 1 - core)
+    for lo in range(2):
+
+        @pl.when(4 * (s // 3) + x_lo != 4 + lo)
+        def _(lo=lo):
+            halo_copy(lo, 1).wait_recv()
+
     at_start = y == 0
     for k in range(2):
         block = jnp.concatenate(
@@ -348,12 +360,11 @@
         return (here + moved) * SCALE
 
     def expand(resid):
-        later = jnp.where(
-            wide_row < 224, pltpu.roll(resid, 224, axis=0), pltpu.roll(resid, 223, axis=0)
-        )
-        later = jnp.where(wide_row == 255, 0.0, later)
         here_t = resid.T
-        later_t = later.T
+        later_t = jnp.where(
+            wide_lane < 224, pltpu.roll(here_t, 224, axis=1), pltpu.roll(here_t, 223, axis=1)
+        )
+        later_t = jnp.where(wide_lane == 255, 0.0, later_t)
         both = jnp.concatenate([here_t, later_t], axis=0)
         r_even[...] = both.astype(BF16)
         r_odd[...] = jnp.concatenate([both[8:], both[:8]], axis=0).astype(BF16)
@@ -565,24 +576,35 @@
         flat = resid_wide[k * 128:(k + 1) * 128, :].T
         resid_ref[:, k * 128:(k + 1) * 128] = flat[0:32, :].astype(BF16)
 
-    finish_energy(1)
-    factors = [factor_rows[1, 0:1, :], factor_rows[2, 0:1, :]]
     for turn in range(2):
         half = tiles.at[turn, pl.ds(0, 31)]
         pltpu.make_async_copy(half, half, t_recv.at[turn]).wait()
+    moved = []
     for half in range(2):
-        steps = [
-            factors[0] * tiles[0, half * 16 + d].astype(F32)
-            + factors[1] * tiles[1, half * 16 + d].astype(F32)
-            for d in range(16)
-        ]
+        for turn in range(2):
+            moved.append(swap_blocks(
+                [tiles[turn, half * 16 + d].astype(F32) for d in range(16)]
+            ))
+    for half in range(2):
         lanes = slice(half * 128, (half + 1) * 128)
-        for u, step in enumerate(swap_blocks(steps)):
-            kernel_ref[u, :, lanes] = step
+        for u in range(16):
+            kernel_ref[u, :, lanes] = factor_rows[1, 0:1, :] * moved[2 * half][u]
+            ker_ref[u, :, lanes] = moved[2 * half + 1][u]
+    finish_energy(1)
+    last = factor_rows[2, 0:1, :]
+    wide_last = jnp.concatenate([last, last], axis=1)
+    for u in range(16):
+        kernel_ref[u] = kernel_ref[u] + wide_last * ker_ref[u]
 
     pltpu.make_async_copy(all_tiles, all_tiles, ker_send).wait()
-    for copy in za_copies + zh_copies + xb_copies + xa_copies + xh_copies + ca_copies + cb_copies + ch_copies:
+    for copy in za_copies + xb_copies + xa_copies + ca_copies + cb_copies:
         copy.wait_send()
+
+    @pl.when(s == 3)
+    def _():
+        for r in range(1, 8):
+            halo_copy(x_lo, r).wait_send()
+
     for copy in zb_copies.values():
         copy.wait_send()
     for turn in range(2):
@@ -638,9 +660,9 @@
             pltpu.VMEM((16, 2048), BF16),
             pltpu.VMEM((16, 16, 256), F32),
             dma((2,)),
-            dma, dma, dma, dma((3,)), dma((3,)), dma, dma,
-            dma((3,)), dma((3,)), dma((3,)), dma((3,)), dma((3,)), dma((3,)), dma((3,)), dma((3,)),
-            dma((3,)), dma((3,)), dma((2,)), dma((2,)), dma((4, 3)), dma((4, 3)), dma((4,)), dma((4,)), dma((4,)), dma((4,)),
+            dma, dma, dma, dma((3,)), dma((3,)), dma((4,)), dma((4,)),
+            dma((3,)), dma((3,)), dma((3,)), dma((3,)), dma((3,)), dma((3,)),
+            dma((7,)), dma((2,)), dma((4, 3)), dma((4, 3)), dma((4,)), dma((4,)), dma((4,)), dma((4,)),
             dma((3,)), dma((3,)), dma((2, 2, 3)), dma((2, 2, 3)), dma((2, 3)), dma((2, 3)),
             dma((2,)), dma((2,)), dma((2, 3)), dma((2, 3)), dma((2,)), dma((2,)), dma((3,)), dma((3,)),
         ],

time: 74.4 us -> 74.1 us (level)
  no operation moved by 1% of the time
where the time goes in v5:
time: 74.1 us; the launch traced here: 74 us
  Pallas kernels  73.3 us (99%)
    pallas_call x1, Pallas kernels, local(): pl.pallas_call(body, out_shape=(jax.ShapeDtypeStruct((16, 16, 256), F32),...  71.5 us
    pallas_call x1, Pallas kernels, local(): pl.pallas_call(finish, out_shape=(jax.ShapeDtypeStruct((16, 16, 256), F32...  1.83 us

profile of v5, /device:TPU:1, one launch (start us, length us, event | category | flops | bytes accessed | tf_op | source)
XLA Modules:
  0.0 74.0 jit_solution(7373547464800034749)
XLA Ops:
  0.6 71.5 %shard_map.50 = (f32[16,16,256]{2,1,0:T(8,128)}, bf16[32,2048]{1,0:T(8,128)(2,1)}) custom-call(bf16[16,2048]{1,0:T(8,128)(2,1)} %bitcast.2, bf16[2048,256]{1,0:T(8,128)(2,1)} %resp_hbm.1, f32[16,16,256]{2,1,0:T(8,128)} %ker_ref.1), custom_call_target="tpu_custom_call" | custom-call | tf_op jit(solution)/shard_map/pallas_call | solution.py:625
  72.1 1.8 %shard_map.51 = (f32[16,16,256]{2,1,0:T(8,128)}, bf16[32,2048]{1,0:T(8,128)(2,1)}) custom-call(f32[16,16,256]{2,1,0:T(8,128)} %get-tuple-element.6.step_ref, f32[16,16,256]{2,1,0:T(8,128)} %ker_ref.1, bf16[32,2048]{1,0:T(8,128)(2,1)} %get-tuple-element.7.resid_in_ref), custom_call_target="tpu_custom_call" | custom-call | tf_op jit(solution)/shard_map/pallas_call | solution.py:673
